TPU v7x, 256 devices: a whole 4x4x8 slice. The times are simulated.
256 devices in a mesh: seq: 2 (over core), tp: 8 (over y, x_lo), section: 16 (over z, x_hi).
Axes of the slice: x: 4 (x_hi: 2, x_lo: 2; x = x_hi * 2 + x_lo), y: 4, z: 8, core: 2. Of those that a mesh axis runs over, the one named last changes fastest.
Arguments:
- hidden: bfloat16 [16384, 4096], P(('seq', 'section'), 'tp'), may hold values from -6 to 6
- gain: bfloat16 [4096], replicated, may hold values from 0.5 to 1.5
- trace_emb: bfloat16 [16384, 1024], P(('seq', 'section'), 'tp')
- counts: int32 [256], P(('seq', 'section')), may hold values from 0 to 4, as said below
- offsets: int32 [256, 4], P(('seq', 'section')), may hold values from 2 to 255, as said below
- w_stretch_kv: bfloat16 [4096, 2048], P(None, 'tp'), may hold values from -0.09375 to 0.09375
- encoder_query_weight: bfloat16 [1024, 1024], P('section'), may hold values from -0.1875 to 0.1875
- encoder_output_weight: bfloat16 [1024, 1024], P('section'), may hold values from -0.1875 to 0.1875
- w_cca_q: bfloat16 [4096, 2048], P(None, 'tp'), may hold values from -0.09375 to 0.09375
- w_cca_kv: bfloat16 [1024, 4096], P(None, 'tp'), may hold values from -0.1875 to 0.1875
- w_cca_o: bfloat16 [2048, 4096], P('tp'), may hold values from -0.1875 to 0.1875
Outputs:
- block_out: bfloat16 [16384, 4096], P(('seq', 'section'), 'tp')
Inputs may be any that keep to these rules, and one draw needn't show every extreme that they name: counts[u] is 0 for the first two stretches; the last stretch has 4. `offsets`: for stretch u >= 2 each offset lies in 2 to u, so a neighbour ends before its stretch; for u < 2 it is 2.
All inputs are finite; a program needn't handle non-finite values.
Results may differ from a plain program's by a relative error of at most 0.02.
Values may be sent and summed in bfloat16 or wider, within the bound.
A program may use at most 128 MiB of HBM per device.

v0:
```python
import math

import jax
import jax.numpy as jnp
from jax import lax
from jax.sharding import PartitionSpec as P

DH = 128
STRETCH_TOKENS = 64
KNB = 4
NLEN = 128


EPS = 1e-05
NEG = -1e30


def passed_along(value, axis, steps):
    count = lax.axis_size(axis)
    initial, last = (max(0, -steps), min(count, count - steps))
    return lax.ppermute(value, axis, [(source, source + steps) for source in range(initial, last)])


def rms_scale(rows, gain):
    wide = rows.astype(jnp.float32)
    inverse = lax.rsqrt(jnp.mean(wide * wide, axis=-1, keepdims=True) + EPS)
    return (wide * inverse * gain.astype(jnp.float32)).astype(jnp.bfloat16)


def encode_neighbours(row_count, stretch_key_values, encoder_query_weight, encoder_output_weight):
    number, keys_n, width = row_count.shape
    heads = encoder_query_weight.shape[1] // DH
    factor = 1.0 / math.sqrt(DH)
    flat = row_count.reshape(number * keys_n, width)
    query = jnp.dot(flat, encoder_query_weight, preferred_element_type=jnp.float32).astype(
        jnp.bfloat16
    )
    query = query.reshape(number, keys_n, heads, DH)
    paired = stretch_key_values.reshape(number, stretch_key_values.shape[1], heads, 2, DH)
    scores = (
        jnp.einsum("cnhd,cmhd->chnm", query, paired[:, :, :, 0], preferred_element_type=jnp.float32)
        * factor
    )
    top = jnp.max(scores, axis=-1, keepdims=True)
    weights = jnp.exp(scores - top)
    probs = (weights / jnp.sum(weights, axis=-1, keepdims=True)).astype(jnp.bfloat16)
    mixed = jnp.einsum(
        "chnm,cmhd->cnhd", probs, paired[:, :, :, 1], preferred_element_type=jnp.float32
    )
    mixed = mixed.astype(jnp.bfloat16).reshape(number * keys_n, heads * DH)
    projected = jnp.dot(mixed, encoder_output_weight, preferred_element_type=jnp.float32)
    return (
        (flat.astype(jnp.float32) + projected).astype(jnp.bfloat16).reshape(number, keys_n, width)
    )


def cross_attend(query, paired, live):
    factor = 1.0 / math.sqrt(DH)
    scores = (
        jnp.einsum("gthd,gkhd->ghtk", query, paired[:, :, :, 0], preferred_element_type=jnp.float32)
        * factor
    )
    mask = live[:, None, None, :]
    scores = jnp.where(mask, scores, NEG)
    top = jnp.max(scores, axis=-1, keepdims=True)
    weights = jnp.where(mask, jnp.exp(scores - top), 0.0)
    total = jnp.sum(weights, axis=-1, keepdims=True)
    anylive = jnp.any(live, axis=-1)[:, None, None, None]
    total = jnp.where(anylive, total, 1.0)
    probs = (weights / total).astype(jnp.bfloat16)
    mixed = jnp.einsum(
        "ghtk,gkhd->gthd", probs, paired[:, :, :, 1], preferred_element_type=jnp.float32
    )
    groups, rows, heads, size = mixed.shape
    return mixed.astype(jnp.bfloat16).reshape(groups, rows, heads * size)


def body(
    hidden,
    gain,
    trace_emb,
    counts,
    offsets,
    w_stretch_kv,
    encoder_query_weight,
    encoder_output_weight,
    w_cca_q,
    w_cca_kv,
    w_cca_o,
):
    tok_rows = hidden.shape[0]
    nstretch = tok_rows // STRETCH_TOKENS
    keys_n = KNB * NLEN
    heads_here = w_cca_q.shape[1] // DH
    width = heads_here * DH
    whole = lax.all_gather(hidden, "tp", axis=1, tiled=True)
    normed = rms_scale(whole, gain)
    stretch_key_values = jnp.dot(normed, w_stretch_kv, preferred_element_type=jnp.float32).astype(
        jnp.bfloat16
    )
    query = jnp.dot(normed, w_cca_q, preferred_element_type=jnp.float32).astype(jnp.bfloat16)
    enc_query_w, enc_out_w = (
        lax.all_gather(encoder_query_weight, "section", axis=0, tiled=True),
        lax.all_gather(encoder_output_weight, "section", axis=0, tiled=True),
    )
    place = lax.axis_index(("seq", "section"))
    stretch_ids = place * nstretch + jnp.arange(nstretch, dtype=jnp.int32)
    source = stretch_ids[:, None] - offsets
    wanted = jnp.stack([source, source + 1], axis=-1).reshape(nstretch * KNB * 2)
    columns = trace_emb.shape[1]
    piece = lax.all_gather(trace_emb, ("seq", "section"), axis=0, tiled=True)
    many = piece.shape[0] // STRETCH_TOKENS
    present = jnp.arange(many, dtype=jnp.int32)
    select = (wanted[:, None] == present[None, :]).astype(jnp.bfloat16)
    fetched = jnp.dot(
        select, piece.reshape(many, STRETCH_TOKENS * columns), preferred_element_type=jnp.float32
    )
    row_count = fetched.astype(jnp.bfloat16).reshape(nstretch * keys_n, columns)
    local_rows, local_kv = (
        lax.all_to_all(row_count, "tp", split_axis=0, concat_axis=1, tiled=True),
        lax.all_to_all(stretch_key_values, "tp", split_axis=0, concat_axis=1, tiled=True),
    )
    portion = local_kv.shape[0] // STRETCH_TOKENS
    encoded_neighbours = encode_neighbours(
        local_rows.reshape(portion, keys_n, local_rows.shape[1]),
        local_kv.reshape(portion, STRETCH_TOKENS, local_kv.shape[1]),
        enc_query_w,
        enc_out_w,
    )
    paired = jnp.dot(
        lax.all_gather(
            encoded_neighbours.reshape(portion * keys_n, encoded_neighbours.shape[2]),
            "tp",
            axis=0,
            tiled=True,
        ),
        w_cca_kv,
        preferred_element_type=jnp.float32,
    ).astype(jnp.bfloat16)
    paired = paired.reshape(nstretch, keys_n, heads_here, 2, DH)
    slot = jnp.arange(keys_n, dtype=jnp.int32) // NLEN
    last_pair, last_count = passed_along(
        (paired[nstretch - 1], counts[nstretch - 1 :]), ("seq", "section"), 1
    )
    ext_pair = jnp.concatenate([last_pair[None], paired], 0)
    ext_count = jnp.concatenate([last_count, counts], 0)
    ext_live = slot[None, :] < ext_count[:, None]
    padded = jnp.concatenate(
        [
            jnp.zeros((1, width), jnp.bfloat16),
            query,
            jnp.zeros((STRETCH_TOKENS - 1, width), jnp.bfloat16),
        ],
        0,
    )
    groups = padded.reshape(nstretch + 1, STRETCH_TOKENS, heads_here, DH)
    mixed = cross_attend(groups, ext_pair, ext_live).reshape((nstretch + 1) * STRETCH_TOKENS, width)
    attended = mixed[1 : tok_rows + 1]
    partial_terms = jnp.dot(attended, w_cca_o, preferred_element_type=jnp.float32)
    summed = lax.psum_scatter(
        partial_terms.astype(jnp.bfloat16), "tp", scatter_dimension=1, tiled=True
    ).astype(jnp.float32)
    return (hidden.astype(jnp.float32) + summed).astype(jnp.bfloat16)


def solution(mesh):
    in_specs = (
        P(("seq", "section"), "tp"),
        P(),
        P(("seq", "section"), "tp"),
        P(("seq", "section")),
        P(("seq", "section"), None),
        P(None, "tp"),
        P("section", None),
        P("section", None),
        P(None, "tp"),
        P(None, "tp"),
        P("tp", None),
    )
    out_specs = P(("seq", "section"), "tp")
    return jax.shard_map(body, mesh=mesh, in_specs=in_specs, out_specs=out_specs, check_vma=False)
```

profile of v0, /device:TPU:1, one launch (start us, length us, event | category | flops | bytes accessed | tf_op | source)
XLA Modules:
  0.0 684.5 jit_solution(17688458238194364746)
XLA Ops:
  6.5 0.7 all-gather.8.cloned.1.call-update
  7.3 0.7 all-gather.6.cloned.1.call-update
  8.1 0.7 all-gather.10.cloned.1.call-update
  8.8 0.5 all-gather.12.cloned.1.call-update
  9.3 0.7 subtract_bitcast_fusion
  10.3 0.7 convert_element_type.69
  11.0 95.1 %all-gather.8.cloned.1.call-done = bf16[512,4096]{1,0:T(8,128)(2,1)} async-done(((bf16[512,512]{1,0:T(8,128)(2,1)}), bf16[512,4096]{1,0:T(8,128)(2,1)}) %all-gather.8.cloned.1.call-update) | async-done | bytes 4194320 | tf_op jit(solution)/shard_map/all_gather | solution.py:96
  106.0 3.2 fusion.2
  109.3 0.2 copy-done.2
  109.5 3.6 fusion.24
  113.1 3.9 all-to-all-start.1
  116.9 79.3 %all-gather.6.cloned.1.call-done = bf16[16384,128]{1,0:T(8,128)(2,1)} async-done(((bf16[512,128]{1,0:T(8,128)(2,1)}), bf16[16384,128]{1,0:T(8,128)(2,1)}) %all-gather.6.cloned.1.call-update) | async-done | bytes 4194320 | tf_op jit(solution)/shard_map/all_gather | solution.py:111
  196.3 7.4 %reshape.114 = bf16[256,8192]{1,0:T(8,128)(2,1)} reshape(bf16[16384,128]{1,0:T(8,128)(2,1)} %all-gather.6.cloned.1.call-done) | data formatting | bytes 8388608 | tf_op jit(solution)/shard_map/reshape | solution.py:116
  203.6 4.0 convolution_convert_fusion
  207.7 1.6 all_to_all.26
  209.2 1.3 copy.28
  210.5 4.0 all-to-all-start
  214.6 0.2 copy.60
  214.8 15.1 %all-to-all-done = bf16[8,512,128]{1,2,0:T(8,128)(2,1)S(1)} async-done(((bf16[8,512,128]{1,2,0:T(8,128)(2,1)}), bf16[8,512,128]{1,2,0:T(8,128)(2,1)S(1)}, u32[]{:S(2)}, u32[]{:S(2)}) %all-to-all-start) | async-done | bytes 1048608 | tf_op jit(solution)/shard_map/all_to_all | solution.py:120
  229.9 1.3 copy.29
  231.2 46.0 %all-gather.10.cloned.1.call-done = bf16[1024,1024]{1,0:T(8,128)(2,1)} async-done(((bf16[64,1024]{1,0:T(8,128)(2,1)}), bf16[1024,1024]{1,0:T(8,128)(2,1)}) %all-gather.10.cloned.1.call-update) | async-done | bytes 2097168 | tf_op jit(solution)/shard_map/all_gather | solution.py:103
  277.1 2.9 fusion.15
  280.0 0.5 convolution_multiply_fusion
  280.5 0.2 fusion.53
  280.7 0.7 copy-done.5
  281.5 3.1 convolution_convert_fusion.3
  284.6 77.2 %all-gather.12.cloned.1.call-done = bf16[1024,1024]{1,0:T(8,128)(2,1)} async-done(((bf16[64,1024]{1,0:T(8,128)(2,1)}), bf16[1024,1024]{1,0:T(8,128)(2,1)}) %all-gather.12.cloned.1.call-update) | async-done | bytes 2097168 | tf_op jit(solution)/shard_map/all_gather | solution.py:104
  361.9 4.2 add_convert_fusion
  366.1 0.6 slice.26
  366.7 2.3 collective-permute-start.1
  369.1 6.2 collective-permute-done.1
  375.4 0.7 pad_add_fusion.1
  376.1 0.2 fusion.51
  376.3 161.1 %all-gather.14.cloned.1.call-done = bf16[4096,1024]{1,0:T(8,128)(2,1)} async-done(((bf16[512,1024]{1,0:T(8,128)(2,1)}), bf16[4096,1024]{1,0:T(8,128)(2,1)}) %all-gather.14.cloned.1.call-update) | async-done | bytes 8388624 | tf_op jit(solution)/shard_map/all_gather | solution.py:131
  537.4 8.2 %convolution_convert_fusion.2 = bf16[4096,512]{0,1:T(8,128)(2,1)S(1)} fusion(bf16[4096,1024]{1,0:T(8,128)(2,1)} %all-gather.14.cloned.1.call-done, bf16[1024,512]{1,0:T(8,128)(2,1)} %param.20), kind=kOutput, calls=%fused_computation.9 | convolution fusion | flops 4297064448 | bytes 13631488 | tf_op jit(solution)/shard_map/dot_general | solution.py:130
  545.6 1.9 copy-done.1
  547.6 0.3 copy.34
  547.8 4.5 collective-permute-start
  552.3 4.2 fusion.27
  556.5 0.2 maximum_maximum_fusion
  556.8 6.4 copy.41
  563.2 7.9 %copy.35 = bf16[8,512,2,2,128]{4,1,2,0,3:T(8,128)(2,1)} copy(bf16[8,512,2,2,128]{1,0,4,3,2:T(8,128)(2,1)} %bitcast.70) | data formatting | bytes 8388608 | tf_op jit(solution)/shard_map/reshape | solution.py:140
  571.1 4.3 fusion.54
  575.4 2.9 fusion.34
  578.3 0.3 copy.37
  578.7 3.2 convolution_convert_fusion.1
  581.9 93.7 %reduce-scatter.2.cloned.1.call-done = bf16[512,512]{1,0:T(8,128)(2,1)} async-done(((bf16[512,4096]{1,0:T(8,128)(2,1)}), bf16[512,512]{1,0:T(8,128)(2,1)}) %reduce-scatter.2.cloned.1.call-update) | async-done | bytes 524304 | tf_op jit(solution)/shard_map/reduce_scatter | solution.py:160
  675.6 2.0 add_convert_fusion.1
  (35 shorter events, 0.8 us)
Async XLA Ops:
  6.5 572.1 %copy-start = (bf16[256,4096]{1,0:T(8,128)(2,1)S(1)}, bf16[256,4096]{1,0:T(8,128)(2,1)}, u32[]{:S(2)}) copy-start(bf16[256,4096]{1,0:T(8,128)(2,1)} %param.21) | copy-start | bytes 6291460
  6.5 99.5 %all-gather.8.cloned.1.call-start = ((), (), s32[]{:S(2)}) async-start(), calls=%async_computation.4 | async-start | bytes 4718592 | tf_op jit(solution)/shard_map/all_gather | solution.py:96
  7.3 189.0 %all-gather.6.cloned.1.call-start = ((), (), s32[]{:S(2)}) async-start(), calls=%async_computation.3 | async-start | bytes 4325376 | tf_op jit(solution)/shard_map/all_gather | solution.py:111
  8.0 269.1 %all-gather.10.cloned.1.call-start = ((), (), s32[]{:S(2)}) async-start(), calls=%async_computation.5 | async-start | bytes 2228224 | tf_op jit(solution)/shard_map/all_gather | solution.py:103
  8.7 353.1 %all-gather.12.cloned.1.call-start = ((), (), s32[]{:S(2)}) async-start(), calls=%async_computation.6 | async-start | bytes 2228224 | tf_op jit(solution)/shard_map/all_gather | solution.py:104
  106.0 3.4 copy-start.2
  113.1 97.5 %all-to-all-start.1 = ((bf16[8,64,256]{2,1,0:T(8,128)(2,1)}), bf16[8,64,256]{2,1,0:T(8,128)(2,1)S(1)}, u32[]{:S(2)}, u32[]{:S(2)}) async-start(bf16[8,64,256]{2,1,0:T(8,128)(2,1)} %bitcast.4), calls=%async_computation.1 | async-start | bytes 524288 | tf_op jit(solution)/shard_map/all_to_all | solution.py:121
  210.5 19.3 %all-to-all-start = ((bf16[8,512,128]{1,2,0:T(8,128)(2,1)}), bf16[8,512,128]{1,2,0:T(8,128)(2,1)S(1)}, u32[]{:S(2)}, u32[]{:S(2)}) async-start(bf16[8,512,128]{1,2,0:T(8,128)(2,1)} %copy.28), calls=%async_computation | async-start | bytes 2097152 | tf_op jit(solution)/shard_map/all_to_all | solution.py:120
  214.6 322.8 %all-gather.14.cloned.1.call-start = ((), (), s32[]{:S(2)}) async-start(), calls=%async_computation.7 | async-start | bytes 9437184 | tf_op jit(solution)/shard_map/all_gather | solution.py:131
  280.5 1.0 copy-start.5
  281.5 80.4 %copy-start.4 = (bf16[512,1024]{1,0:T(8,128)(2,1)S(1)}, bf16[512,1024]{1,0:T(8,128)(2,1)}, u32[]{:S(2)}) copy-start(bf16[512,1024]{1,0:T(8,128)(2,1)} %copy.29) | copy-start | bytes 3145732
  361.9 4.3 copy-start.6
  366.1 309.6 %reduce-scatter.2.cloned.1.call-start = ((), (), s32[]{:S(2)}) async-start(), calls=%async_computation.8 | async-start | bytes 4718592 | tf_op jit(solution)/shard_map/reduce_scatter | solution.py:160
  366.7 8.7 %collective-permute-start.1 = (s32[1]{0:T(128)}, s32[1]{0:T(128)}, u32[]{:S(2)}, u32[]{:S(2)}) collective-permute-start(s32[1]{0:T(128)} %slice.26), channel_id=1, source_target_pairs={{0,1},{1,2},{2,3},{3,4},{4,5},{5,6},{6,7},{7,8},{8,9},{9,10},{10,1... | collective-permute-start | bytes 20 | tf_op jit(solution)/shard_map/ppermute | solution.py:21
  545.6 2.0 copy-start.1
  547.8 23.2 %collective-permute-start = (bf16[512,2,2,128]{3,0,1,2:T(8,128)(2,1)S(1)}, bf16[512,2,2,128]{3,0,1,2:T(8,128)(2,1)}, u32[]{:S(2)}, u32[]{:S(2)}) collective-permute-start(bf16[512,2,2,128]{3,0,1,2:T(8,128)(2,1)S(1)} %copy.34), channel_id=1, source_target_pairs={{0,1},{1,2},{2,3},{3,4},{4,5},{5,6},{6,7},{7,8},{8,9},{9,10},{10,1... | collective-permute-start | bytes 1572872 | tf_op jit(solution)/shard_map/ppermute | solution.py:21
  581.9 93.7 %copy-start.3 = (bf16[512,512]{1,0:T(8,128)(2,1)S(1)}, bf16[512,512]{1,0:T(8,128)(2,1)}, u32[]{:S(2)}) copy-start(bf16[512,512]{1,0:T(8,128)(2,1)} %param.11) | copy-start | bytes 1572868
Sparse Core Ops, SparseCore 0:
  9.2 96.8 all-gather.7
  108.8 87.4 all-gather.5
  198.9 78.2 all-gather.9
  279.6 82.2 all-gather.11
  366.2 171.1 all-gather.13
  582.1 93.5 reduce-scatter.1
where the time goes:
time: 685 us; the launch traced here: 684 us
  waiting for transfers between devices  576 us (84%)
  matrix products  41 us (6%)
  local copies, waits for them, and re-layouts  30.5 us (4%)
  starting transfers between devices  14.9 us (2%)
  between operations  13.7 us (2%)
  other arithmetic  8.01 us (1%)
    all_gather x1, waiting for transfers between devices, body(): lax.all_gather(encoded_neighbours.reshape(portion * keys_n, encoded_neigh...  161 us
    all_gather x1, waiting for transfers between devices, body(): whole = lax.all_gather(hidden, 'tp', axis=1, tiled=True)  95.1 us
    reduce_scatter x1, waiting for transfers between devices, body(): lax.psum_scatter(partial_terms.astype(jnp.bfloat16), 'tp', scatter_dimens...  93.7 us
    all_gather x1, waiting for transfers between devices, body(): piece = lax.all_gather(trace_emb, ('seq', 'section'), axis=0, tiled=True)  79.3 us
    all_gather x1, waiting for transfers between devices, body(): lax.all_gather(encoder_output_weight, 'section', axis=0, tiled=True)  77.2 us
    all_gather x1, waiting for transfers between devices, body(): lax.all_gather(encoder_query_weight, 'section', axis=0, tiled=True)  46 us
    all_to_all x1, waiting for transfers between devices, body(): lax.all_to_all(row_count, 'tp', split_axis=0, concat_axis=1, tiled=True)  15.1 us
  transfers between devices with their start and end apart: 10, of which 8 were waited for; matrix products, arithmetic and copies ran while one was open for 7% of the time, Pallas kernels for 0%

commit v1 on v0

v1 whole, which is shorter than its diff:
```python
import functools
import math

import jax
import jax.numpy as jnp
from jax import lax
from jax.experimental import pallas as pl
from jax.experimental.pallas import tpu as pltpu
from jax.sharding import PartitionSpec as P

MESH = pl.DeviceIdType.MESH
BF = jnp.bfloat16
F32 = jnp.float32
EPS = 1e-05
NEG = -1e30
FACTOR = 1.0 / math.sqrt(128)
TP = 8
PLACES = 32


def remote(src, dst, send, recv, to):
    return pltpu.make_async_remote_copy(
        src_ref=src, dst_ref=dst, send_sem=send, recv_sem=recv, device_id=to, device_id_type=MESH
    )


def dot(a, b):
    return jnp.dot(a, b, preferred_element_type=F32)


def dot_t(a, b):
    return lax.dot_general(a, b, (((1,), (1,)), ((), ())), preferred_element_type=F32)


class Here:
    def __init__(self):
        self.c = lax.axis_index("seq")
        self.t = lax.axis_index("tp")
        self.s = lax.axis_index("section")
        self.y, self.xl = self.t // 2, self.t % 2
        self.z, self.xh = self.s // 2, self.s % 2
        self.p = self.c * 16 + self.s
        c, t, s = self.c, self.t, self.s
        self.yp = (c, self.slot(1, 0), s)
        self.ym = (c, self.slot(3, 0), s)
        self.xp = (c, self.slot(0, 1), s)
        self.zp = (c, t, ((self.z + 1) % 8) * 2 + self.xh)
        self.zm = (c, t, ((self.z + 7) % 8) * 2 + self.xh)
        self.x2 = (c, t, self.z * 2 + 1 - self.xh)
        self.core = (1 - c, t, s)
        before, after = (self.p + PLACES - 1) % PLACES, (self.p + 1) % PLACES
        self.before = (before // 16, before % 16)
        self.after = (after // 16, after % 16)

    def slot(self, dy, other):
        xl = 1 - self.xl if other else self.xl
        return ((self.y + dy) % 4) * 2 + xl

    def tp_peer(self, i):
        return (self.t + i) % TP

    def at_tp(self, t):
        return (self.c, t, self.s)

    def last_before(self):
        return (self.before[0], TP - 1, self.before[1])

    def at_after(self, t):
        return (self.after[0], t, self.after[1])


class Gather:
    def __init__(self, here, region, own, send, recv, arrived):
        self.here, self.region, self.own = here, region, own
        self.send_sem, self.recv_sem, self.arrived = send, recv, arrived
        self.sent = []

    def send(self, m, to, slot, part, half=None, own=False):
        src = self.own(part) if own else self.region(slot, part, half)
        copy = remote(src, self.region(slot, part, half), self.send_sem.at[m], self.recv_sem.at[m], to)
        copy.start()
        self.sent.append(copy)

    def wait(self, m, slot, part, half=None):
        ref = self.region(slot, part, half)
        remote(ref, ref, self.send_sem.at[m], self.recv_sem.at[m], self.here.xp).wait_recv()

    def begin(self, part):
        h = self.here
        me = h.t
        if part == 0:
            self.send(0, h.xp, me, 0, own=True)
            self.send(1, h.yp, me, 0, own=True)
            self.send(2, h.ym, me, 0, own=True)
        else:
            self.send(4, h.yp, me, 1, own=True)
            self.send(5, h.ym, me, 1, own=True)
            self.send(3, h.xp, me, 1, own=True)

    def steps(self):
        h = self.here
        slot = h.slot
        self.wait(0, slot(0, 1), 0)
        self.send(6, h.yp, slot(0, 1), 0)
        self.send(7, h.ym, slot(0, 1), 0)
        self.arrived(slot(0, 1), 0, 0)
        yield
        self.wait(4, slot(3, 0), 1)
        self.send(12, h.xp, slot(3, 0), 1)
        self.send(14, h.yp, slot(3, 0), 1, 0)
        self.arrived(slot(3, 0), 1, 1)
        yield
        self.wait(5, slot(1, 0), 1)
        self.send(13, h.xp, slot(1, 0), 1)
        self.send(15, h.ym, slot(1, 0), 1, 1)
        self.arrived(slot(1, 0), 1, 2)
        yield
        self.wait(1, slot(3, 0), 0)
        self.send(8, h.yp, slot(3, 0), 0, 0)
        self.arrived(slot(3, 0), 0, 3)
        yield
        self.wait(2, slot(1, 0), 0)
        self.send(9, h.ym, slot(1, 0), 0, 1)
        self.arrived(slot(1, 0), 0, 4)
        yield
        self.wait(3, slot(0, 1), 1)
        self.arrived(slot(0, 1), 1, 5)
        yield
        self.wait(14, slot(2, 0), 1, 0)
        self.send(16, h.xp, slot(2, 0), 1, 0)
        self.wait(15, slot(2, 0), 1, 1)
        self.send(17, h.xp, slot(2, 0), 1, 1)
        self.arrived(slot(2, 0), 1, 6)
        yield
        self.wait(6, slot(3, 1), 0)
        self.send(10, h.yp, slot(3, 1), 0, 0)
        self.arrived(slot(3, 1), 0, 7)
        yield
        self.wait(7, slot(1, 1), 0)
        self.send(11, h.ym, slot(1, 1), 0, 1)
        self.arrived(slot(1, 1), 0, 8)
        yield
        self.wait(8, slot(2, 0), 0, 0)
        self.wait(9, slot(2, 0), 0, 1)
        self.arrived(slot(2, 0), 0, 9)
        yield
        self.wait(12, slot(3, 1), 1)
        self.arrived(slot(3, 1), 1, 10)
        yield
        self.wait(13, slot(1, 1), 1)
        self.arrived(slot(1, 1), 1, 11)
        yield
        self.wait(10, slot(2, 1), 0, 0)
        self.wait(11, slot(2, 1), 0, 1)
        self.arrived(slot(2, 1), 0, 12)
        yield
        self.wait(16, slot(2, 1), 1, 0)
        self.wait(17, slot(2, 1), 1, 1)
        self.arrived(slot(2, 1), 1, 13)

    def order(self):
        s = self.here.slot
        return [
            (s(0, 1), 0), (s(3, 0), 1), (s(1, 0), 1), (s(3, 0), 0), (s(1, 0), 0), (s(0, 1), 1), (s(2, 0), 1),
            (s(3, 1), 0), (s(1, 1), 0), (s(2, 0), 0), (s(3, 1), 1), (s(1, 1), 1), (s(2, 1), 0), (s(2, 1), 1),
        ]

    def finish(self):
        for copy in self.sent:
            copy.wait_send()


class Ring:
    OFFSET = [0, 7, 1, 6, 2, 5, 3, 4]

    def __init__(self, here, region, sems, flip):
        self.here, self.region, self.flip = here, region, flip
        self.send_sem, self.recv_sem, self.core_send, self.core_recv = sems
        self.sent = []

    def push(self, way, r):
        h = self.here
        z = (h.z + (8 - r if way == 0 else r)) % 8
        ref = self.region(z, h.c)
        m = way * 4 + r
        copy = remote(ref, ref, self.send_sem.at[m], self.recv_sem.at[m], h.zp if way == 0 else h.zm)
        copy.start()
        self.sent.append(copy)

    def share(self, k):
        h = self.here
        ref = self.region((h.z + self.dz(k)) % 8, h.c)
        copy = remote(ref, ref, self.core_send.at[k], self.core_recv.at[k], h.core)
        copy.start()
        self.sent.append(copy)

    def dz(self, k):
        return self.OFFSET[k] if not self.flip else (8 - self.OFFSET[k]) % 8

    def wait(self, way, r, k):
        h = self.here
        ref = self.region((h.z + self.dz(k)) % 8, h.c)
        m = way * 4 + r
        remote(ref, ref, self.send_sem.at[m], self.recv_sem.at[m], h.zp).wait_recv()

    def steps(self):
        first, second = (1, 0) if self.flip else (0, 1)
        self.push(first, 0)
        self.push(second, 0)
        self.share(0)
        yield
        for r in range(3):
            self.wait(first, r, 1 + 2 * r)
            self.push(first, r + 1)
            self.share(1 + 2 * r)
            self.wait(second, r, 2 + 2 * r)
            if r < 2:
                self.push(second, r + 1)
            self.share(2 + 2 * r)
            yield
        self.wait(first, 3, 7)
        self.share(7)
        yield

    def collect(self):
        h = self.here
        for k in range(8):
            ref = self.region((h.z + self.dz(k)) % 8, 1 - h.c)
            remote(ref, ref, self.core_send.at[k], self.core_recv.at[k], h.core).wait_recv()

    def finish(self):
        for copy in self.sent:
            copy.wait_send()


def advance(steps, n=1):
    for _ in range(n):
        next(steps, None)


def kernel(
    hidden, gain, trace, counts, offsets, w_skv, w_eq, w_eo, w_cq, w_ckv, w_co, out,
    hid, wproj, acc, ssq, kv_s, q_s, tr, picked, rows, enc_w, wck, woc, kvx, qx, qh, eq, ea, enc,
    att_own, attg, tail, attb,
    local, h_send, h_recv, k_send, k_recv, a_send, a_recv, kc_send, kc_recv,
    x_send, x_recv, tr_ss, tr_rs, tr_cs, tr_cr, e_ss, e_rs, e_cs, e_cr, o_ss, o_rs, o_cs, o_cr,
    p_send, p_recv, halo_send, halo_recv, tail_send, tail_recv,
):
    h = Here()
    c, t, s, z, xh, p = h.c, h.t, h.s, h.z, h.xh, h.p
    is_last = t == TP - 1

    barrier = pltpu.get_barrier_semaphore()
    greet = [h.at_tp(h.tp_peer(i)) for i in range(1, TP)]
    greet += [h.zp, h.zm, h.x2, h.core, h.last_before()]
    for device in greet:
        pl.semaphore_signal(barrier, inc=1, device_id=device, device_id_type=MESH)

    @pl.when(is_last)
    def _():
        for other in range(TP):
            pl.semaphore_signal(barrier, inc=1, device_id=h.at_after(other), device_id_type=MESH)

    pl.semaphore_wait(barrier, len(greet) + TP * (t // (TP - 1)))

    started = []

    def bring(src, dst, i):
        copy = pltpu.make_async_copy(src, dst, local.at[i])
        copy.start()
        return copy

    def hid_region(slot, part, half):
        if half is None:
            return hid.at[slot, pl.ds(part * 256, 256)]
        return hid.at[slot, pl.ds(part * 256 + half * 128, 128)]

    first = []

    def project(slot, part, index):
        here = pl.ds(part * 256, 256)
        wide = hid[slot, here, :].astype(F32)
        squares = jnp.sum(wide * wide, axis=-1, keepdims=True)
        scaled = (wide * gain[slot]).astype(BF)
        w = wproj[pl.ds(pl.multiple_of(slot * 512, 512), 512), :]
        product = dot(scaled, w)
        if index is None:
            ssq[here, :] = squares
            acc[here, :] = product
        else:
            ssq[here, :] += squares
            acc[here, :] += product

    gather_h = Gather(
        h, hid_region, lambda part: hidden.at[pl.ds(part * 256, 256)], h_send, h_recv, project
    )
    gather_h.begin(0)
    gather_h.begin(1)

    mine = pl.ds(p * 8, 8)
    other = pl.ds((p + 1 - 2 * xh) * 8, 8)
    trace_x2 = remote(trace, tr.at[mine], x_send.at[0], x_recv.at[0], h.x2)
    trace_x2.start()
    own_trace = bring(trace, tr.at[mine], 0)
    own_hid = bring(hidden, hid.at[t], 1)
    own_skv = bring(w_skv, wproj.at[:, pl.ds(0, 256)], 2)
    own_cq = bring(w_cq, wproj.at[:, pl.ds(256, 256)], 3)
    halves = pl.ds(c * 32, 32)
    own_eq = bring(w_eq.at[halves], enc_w.at[0, s, c], 4)
    own_eo = bring(w_eo.at[halves], enc_w.at[1, s, c], 5)
    own_ckv = bring(w_ckv, wck.at[t], 6)
    slice_rows = pl.ds(z * 32 + c * 16, 16)
    own_co = bring(
        w_co.at[slice_rows, pl.ds(pl.multiple_of(t * 512, 512), 512)], woc.at[t, z * 2 + c], 7
    )

    trace_in = remote(tr.at[other], tr.at[other], x_send.at[0], x_recv.at[0], h.x2)
    own_trace.wait()
    trace_in.wait_recv()
    ring_t = Ring(
        h, lambda zz, cc: tr.at[pl.ds((cc * 16 + zz * 2) * 8, 16)],
        (tr_ss, tr_rs, tr_cs, tr_cr), False,
    )
    steps_t = ring_t.steps()
    advance(steps_t)

    eq_x2 = remote(w_eq.at[halves], enc_w.at[0, s, c], x_send.at[1], x_recv.at[1], h.x2)
    eo_x2 = remote(w_eo.at[halves], enc_w.at[1, s, c], x_send.at[2], x_recv.at[2], h.x2)
    eq_x2.start()
    eo_x2.start()
    pushes = []
    for i in range(1, TP):
        to = h.tp_peer(i)
        copy = remote(
            w_co.at[slice_rows, pl.ds(pl.multiple_of(to * 512, 512), 512)], woc.at[t, z * 2 + c],
            p_send.at[0, i], p_recv.at[0, i], h.at_tp(to),
        )
        copy.start()
        pushes.append(copy)

    own_hid.wait()
    own_skv.wait()
    own_cq.wait()
    project(t, 0, None)
    project(t, 1, None)

    steps_h = gather_h.steps()
    advance(steps_h, 3)
    advance(steps_t)
    advance(steps_h, 3)
    advance(steps_t)
    own_eq.wait()
    own_eo.wait()
    s_other = z * 2 + 1 - xh
    for w in range(2):
        ref = enc_w.at[w, s_other, c]
        remote(ref, ref, x_send.at[1 + w], x_recv.at[1 + w], h.x2).wait_recv()
    ring_e = Ring(
        h, lambda zz, cc: enc_w.at[:, pl.ds(zz * 2, 2), cc], (e_ss, e_rs, e_cs, e_cr), True
    )
    steps_e = ring_e.steps()
    advance(steps_h, 2)
    advance(steps_t)
    advance(steps_e)
    advance(steps_h, 3)
    advance(steps_t)
    advance(steps_e)
    advance(steps_h, 4)

    inverse = lax.rsqrt(ssq[...] * (1.0 / 4096) + EPS)
    projected = (acc[...] * inverse).astype(BF)
    kv_s[...] = projected[:, :256]
    q_s[0:512, :] = projected[:, 256:]
    q_s[512:576, :] = jnp.zeros((64, 256), BF)
    for i in range(1, TP):
        to = h.tp_peer(i)
        copy = remote(
            kv_s.at[pl.ds(pl.multiple_of(to * 64, 64), 64)], kvx.at[t],
            p_send.at[1, i], p_recv.at[1, i], h.at_tp(to),
        )
        copy.start()
        pushes.append(copy)
    kvx[t] = kv_s[pl.ds(pl.multiple_of(t * 64, 64), 64), :]

    ring_t.collect()

    def pick(owner):
        for k in range(4):
            at = p * 8 + owner - offsets[owner, k]
            at = jnp.minimum(jnp.maximum(at, 0), 254)
            picked[owner, 128 * k : 128 * k + 64, :] = tr[at]
            picked[owner, 128 * k + 64 : 128 * k + 128, :] = tr[at + 1]

    columns = pl.ds(pl.multiple_of(t * 128, 128), 128)
    for i in range(1, TP):
        to = h.tp_peer(i)
        pick(to)
        copy = remote(
            picked.at[to], rows.at[:, columns], p_send.at[2, i], p_recv.at[2, i], h.at_tp(to)
        )
        copy.start()
        pushes.append(copy)
    pick(t)
    rows[:, columns] = picked[t]

    for i in range(1, TP):
        to = h.tp_peer(i)
        copy = remote(
            q_s.at[pl.ds(pl.multiple_of(to * 64 + 48, 16), 80)], qx.at[t],
            p_send.at[3, i], p_recv.at[3, i], h.at_tp(to),
        )
        copy.start()
        pushes.append(copy)
    qx[t] = q_s[pl.ds(pl.multiple_of(t * 64 + 48, 16), 80), :]
    halo = remote(q_s.at[pl.ds(0, 64)], qh.at[t], halo_send.at[0], halo_recv.at[t], h.last_before())
    halo.start()
    pushes.append(halo)

    advance(steps_e)

    def wck_region(slot, part, half):
        base = c * 512 + part * 256
        if half is None:
            return wck.at[slot, pl.ds(base, 256)]
        return wck.at[slot, pl.ds(base + half * 128, 128)]

    shared = []

    def share(slot, part, index):
        ref = wck_region(slot, part, None)
        copy = remote(ref, ref, kc_send.at[index], kc_recv.at[index], h.core)
        copy.start()
        shared.append(copy)

    own_ckv.wait()
    gather_k = Gather(
        h, wck_region, lambda part: wck.at[t, pl.ds(c * 512 + part * 256, 256)], k_send, k_recv, share
    )
    gather_k.begin(0)
    gather_k.begin(1)
    steps_k = gather_k.steps()

    own_co.wait()
    for i in range(1, TP):
        ref = woc.at[h.tp_peer(TP - i), z * 2 + c]
        remote(ref, ref, p_send.at[0, i], p_recv.at[0, i], h.core).wait_recv()
    ring_o = Ring(h, lambda zz, cc: woc.at[:, zz * 2 + cc], (o_ss, o_rs, o_cs, o_cr), False)
    steps_o = ring_o.steps()

    advance(steps_e, 2)
    advance(steps_o)
    for i in range(1, TP):
        came = h.tp_peer(TP - i)
        ref = rows.at[:, pl.ds(pl.multiple_of(came * 128, 128), 128)]
        remote(ref, ref, p_send.at[2, i], p_recv.at[2, i], h.core).wait_recv()
    ring_e.collect()
    advance(steps_k, 2)

    for n in range(4):
        cols = slice(256 * n, 256 * (n + 1))
        eq[:, cols] = dot(rows[...], enc_w[0, :, :, :, cols].reshape(1024, 256)).astype(BF)
    for i in range(1, TP):
        came = h.tp_peer(TP - i)
        ref = kvx.at[came]
        remote(ref, ref, p_send.at[1, i], p_recv.at[1, i], h.core).wait_recv()
    advance(steps_k, 1)
    for e in range(8):
        cols = slice(128 * e, 128 * (e + 1))
        scores = dot_t(eq[:, cols], kvx[e, :, :128]) * FACTOR
        top = jnp.max(scores, axis=-1, keepdims=True)
        weights = jnp.exp(scores - top)
        probs = (weights / jnp.sum(weights, axis=-1, keepdims=True)).astype(BF)
        ea[:, cols] = dot(probs, kvx[e, :, 128:]).astype(BF)
        advance(steps_k, 1)
        if e % 2:
            advance(steps_o)
    for n in range(4):
        cols = slice(256 * n, 256 * (n + 1))
        update = dot(ea[...], enc_w[1, :, :, :, cols].reshape(1024, 256))
        enc[:, cols] = (rows[:, cols].astype(F32) + update).astype(BF)
    advance(steps_k, 3)

    for i in range(1, TP):
        came = h.tp_peer(TP - i)
        ref = qx.at[came]
        remote(ref, ref, p_send.at[3, i], p_recv.at[3, i], h.core).wait_recv()

    @pl.when(is_last)
    def _():
        for j in range(TP):
            ref = qh.at[j]
            remote(ref, ref, halo_send.at[0], halo_recv.at[j], h.core).wait_recv()
            qx[j, 16:80, :] = qh[j]

    for index, (slot, part) in enumerate(gather_k.order()):
        ref = wck.at[slot, pl.ds((1 - c) * 512 + part * 256, 256)]
        remote(ref, ref, kc_send.at[index], kc_recv.at[index], h.core).wait_recv()

    live_keys = counts[t] * 128
    lane = lax.broadcasted_iota(jnp.int32, (80, 512), 1)
    mask = lane < live_keys
    row = lax.broadcasted_iota(jnp.int32, (80, 128), 0)
    keep = (row >= 15) & (row < 79)

    def att_region(slot, part, half):
        if half is None:
            return attg.at[slot, :, pl.ds(part * 1024, 1024)]
        return attg.at[slot, :, pl.ds(part * 1024 + half * 512, 512)]

    gather_a = Gather(
        h, att_region, lambda part: att_own.at[:, pl.ds(part * 1024, 1024)], a_send, a_recv,
        lambda slot, part, index: None,
    )
    for j in range(TP):
        pair = dot(enc[...], wck[j]).astype(BF)
        for half in range(2):
            key = pair[:, 256 * half : 256 * half + 128]
            value = pair[:, 256 * half + 128 : 256 * half + 256]
            query = qx[j, :, 128 * half : 128 * half + 128]
            scores = jnp.where(mask, dot_t(query, key) * FACTOR, NEG)
            top = jnp.max(scores, axis=-1, keepdims=True)
            weights = jnp.where(mask, jnp.exp(scores - top), 0.0)
            total = jnp.sum(weights, axis=-1, keepdims=True)
            total = jnp.where(total > 0.0, total, 1.0)
            probs = (weights / total).astype(BF)
            mixed = jnp.where(keep, dot(probs, value), 0.0).astype(BF)
            at = 256 * j + 128 * half
            att_own[:, at : at + 128] = mixed
        if j == 3:
            gather_a.begin(0)
    gather_a.begin(1)

    @pl.when(is_last)
    def _():
        for j in range(TP):
            remote(
                att_own.at[pl.ds(16, 64), pl.ds(256 * j, 256)], tail.at[j],
                tail_send.at[j], tail_recv.at[0], h.at_after(j),
            ).start()

    steps_a = gather_a.steps()
    advance(steps_a, 3)
    remote(tail.at[t], tail.at[t], tail_send.at[0], tail_recv.at[0], h.core).wait_recv()
    for i in range(1, TP):
        copy = remote(tail.at[t], tail.at[t], p_send.at[4, i], p_recv.at[4, i], h.at_tp(h.tp_peer(i)))
        copy.start()
        pushes.append(copy)
    advance(steps_a, 11)
    attg[t] = att_own[...]
    for i in range(1, TP):
        ref = tail.at[h.tp_peer(TP - i)]
        remote(ref, ref, p_send.at[4, i], p_recv.at[4, i], h.core).wait_recv()
    ring_o.collect()

    for j in range(TP):
        attb[0:64, 256 * j : 256 * (j + 1)] = jnp.where(p > 0, tail[j].astype(F32), 0.0).astype(BF)
    for v in range(TP):
        if v:
            attb[64 * v : 64 * v + 64, :] = attg[v - 1, 16:80, :]
        attb[64 * v + 48 : 64 * v + 64, :] += attg[v, 0:16, :]
    for n in range(2):
        cols = slice(256 * n, 256 * (n + 1))
        update = dot(attb[...], woc[:, :, :, cols].reshape(2048, 256))
        out[:, cols] = (hid[t, :, cols].astype(F32) + update).astype(BF)

    gather_h.finish()
    gather_k.finish()
    gather_a.finish()
    ring_t.finish()
    ring_e.finish()
    ring_o.finish()
    trace_x2.wait_send()
    eq_x2.wait_send()
    eo_x2.wait_send()
    for copy in shared + pushes:
        copy.wait_send()

    @pl.when(is_last)
    def _():
        for j in range(TP):
            remote(
                att_own.at[pl.ds(16, 64), pl.ds(256 * j, 256)], tail.at[j],
                tail_send.at[j], tail_recv.at[0], h.at_after(j),
            ).wait_send()


def body(hidden, gain, trace, counts, offsets, w_skv, w_eq, w_eo, w_cq, w_ckv, w_co):
    any_ = pl.BlockSpec(memory_space=pl.ANY)
    vmem = pl.BlockSpec(memory_space=pltpu.VMEM)
    smem = pl.BlockSpec(memory_space=pltpu.SMEM)
    dma = pltpu.SemaphoreType.DMA
    v = pltpu.VMEM
    scratch = [
        v((8, 512, 512), BF),
        v((4096, 512), BF),
        v((512, 512), F32),
        v((512, 1), F32),
        v((512, 256), BF),
        v((576, 256), BF),
        v((256, 64, 128), BF),
        v((8, 512, 128), BF),
        v((512, 1024), BF),
        v((2, 16, 2, 32, 1024), BF),
        v((8, 1024, 512), BF),
        v((8, 16, 16, 512), BF),
        v((8, 64, 256), BF),
        v((8, 80, 256), BF),
        v((8, 64, 256), BF),
        v((512, 1024), BF),
        v((512, 1024), BF),
        v((512, 1024), BF),
        v((80, 2048), BF),
        v((8, 80, 2048), BF),
        v((8, 64, 256), BF),
        v((512, 2048), BF),
        dma((8,)),
        dma((18,)), dma((18,)), dma((18,)), dma((18,)), dma((18,)), dma((18,)), dma((14,)), dma((14,)),
        dma((3,)), dma((3,)),
        dma((8,)), dma((8,)), dma((8,)), dma((8,)),
        dma((8,)), dma((8,)), dma((8,)), dma((8,)),
        dma((8,)), dma((8,)), dma((8,)), dma((8,)),
        dma((5, 8)), dma((5, 8)),
        dma((1,)), dma((8,)), dma((8,)), dma((1,)),
    ]
    return pl.pallas_call(
        kernel,
        out_shape=jax.ShapeDtypeStruct((512, 512), BF),
        in_specs=[any_, vmem, any_, smem, smem, any_, any_, any_, any_, any_, any_],
        out_specs=vmem,
        scratch_shapes=scratch,
        compiler_params=pltpu.CompilerParams(
            collective_id=0, has_side_effects=True, vmem_limit_bytes=58 << 20
        ),
        cost_estimate=pl.CostEstimate(flops=11_000_000_000, bytes_accessed=14_000_000, transcendentals=1_000_000),
    )(
        hidden, gain.astype(F32).reshape(8, 1, 512), trace.reshape(8, 64, 128), counts, offsets,
        w_skv, w_eq, w_eo, w_cq, w_ckv, w_co,
    )


def solution(mesh):
    place = ("seq", "section")
    in_specs = (
        P(place, "tp"), P(), P(place, "tp"), P(place), P(place, None), P(None, "tp"),
        P("section", None), P("section", None), P(None, "tp"), P(None, "tp"), P("tp", None),
    )
    return jax.shard_map(body, mesh=mesh, in_specs=in_specs, out_specs=P(place, "tp"), check_vma=False)
```

time: 685 us -> 154 us (0.22)
  waiting for transfers between devices: 576 us -> 0 us
  Pallas kernels: 0 us -> 149 us
  matrix products: 41 us -> 0 us
  local copies, waits for them, and re-layouts: 30.5 us -> 3.22 us
  starting transfers between devices: 14.9 us -> 0 us
  between operations: 13.7 us -> 0.01 us
    all_gather x5 -> x0, waiting for transfers between devices: 459 us -> none  [the longest x1 161 us: body(): lax.all_gather(encoded_neighbours.reshape(portion * keys_n, encoded_neigh...]
    pallas_call x0 -> x1, Pallas kernels: none -> 149 us  [body(): pl.pallas_call(kernel, out_shape=jax.ShapeDtypeStruct((512, 512), BF), in...]
    reduce_scatter x1 -> x0, waiting for transfers between devices: 93.7 us -> none  [body(): lax.psum_scatter(partial_terms.astype(jnp.bfloat16), 'tp', scatter_dimens...]
    dot_general x10 -> x0, matrix products: 36.7 us -> none  [the longest x1 8.17 us: body(): jnp.dot(lax.all_gather(encoded_neighbours.reshape(portion * keys_n, encod...]
    reshape x3 -> x0, local copies, waits for them, and re-layouts: 15.3 us -> none  [the longest x1 7.89 us: body(): paired = paired.reshape(nstretch, keys_n, heads_here, 2, DH)]
    all_to_all x2 -> x0, waiting for transfers between devices: 15.1 us -> none  [the longest x1 15.1 us: body(): lax.all_to_all(row_count, 'tp', split_axis=0, concat_axis=1, tiled=True)]
    all_to_all x2 -> x0, starting transfers between devices: 7.88 us -> none  [the longest x1 4.02 us: body(): lax.all_to_all(row_count, 'tp', split_axis=0, concat_axis=1, tiled=True)]
  transfers between devices with their start and end apart: 10 -> 0, of which waited for: 8 -> 0; matrix products, arithmetic and copies ran while one was open for 7% -> 0% of each run, Pallas kernels for 0% -> 0%
where the time goes in v1:
time: 154 us; the launch traced here: 153 us
  Pallas kernels  149 us (97%)
  local copies, waits for them, and re-layouts  3.22 us (2%)
    pallas_call x1, Pallas kernels, body(): pl.pallas_call(kernel, out_shape=jax.ShapeDtypeStruct((512, 512), BF), in...  149 us
    unnamed x2, local copies, waits for them, and re-layouts  3.22 us

profile of v1, /device:TPU:1, one launch (start us, length us, event | category | flops | bytes accessed | tf_op | source)
XLA Modules:
  0.0 153.4 jit_solution(4351781179697033514)
XLA Ops:
  0.0 1.3 copy.12.offsets
  1.3 1.3 reshape.11
  2.7 148.9 %shard_map.109 = bf16[512,512]{1,0:T(8,128)(2,1)} custom-call(bf16[512,512]{1,0:T(8,128)(2,1)} %hidden.1, f32[8,1,512]{2,1,0:T(1,128)} %bitcast.2, bf16[8,64,128]{2,1,0:T(8,128)(2,1)} %bitcast.3, s32[8]{0:T(128)} %counts.1, s32[8,4]{1,0:T(8,128)} %copy.12.offsets, bf16[4096,256]{1,0:T(8,128)(2,1)} %w_skv.1, bf16[64,1024]{1,0:T(8,128)(2,1)} %w_eq.1, ...), custom_call_target="tpu_custom_call" | custom-call | flops 11000000512 | bytes 14000000 | tf_op jit(solution)/shard_map/pallas_call | solution.py:625
  151.5 1.9 %copy.14 = bf16[512,512]{1,0:T(8,128)(2,1)} copy(bf16[512,512]{1,0:T(8,128)(2,1)} %shard_map.109) | data formatting | bytes 1048576

commit v2 on v1

v2 whole, which is shorter than its diff:
```python
import functools
import math

import jax
import jax.numpy as jnp
from jax import lax
from jax.experimental import pallas as pl
from jax.experimental.pallas import tpu as pltpu
from jax.sharding import PartitionSpec as P

MESH = pl.DeviceIdType.MESH
BF = jnp.bfloat16
F32 = jnp.float32
EPS = 1e-05
NEG = -1e30
FACTOR = 1.0 / math.sqrt(128)
TP = 8
PLACES = 32


def remote(src, dst, send, recv, to):
    return pltpu.make_async_remote_copy(
        src_ref=src, dst_ref=dst, send_sem=send, recv_sem=recv, device_id=to, device_id_type=MESH
    )


def dot(a, b):
    return jnp.dot(a, b, preferred_element_type=F32)


def dot_t(a, b):
    return lax.dot_general(a, b, (((1,), (1,)), ((), ())), preferred_element_type=F32)


class Here:
    def __init__(self):
        self.c = lax.axis_index("seq")
        self.t = lax.axis_index("tp")
        self.s = lax.axis_index("section")
        self.y, self.xl = self.t // 2, self.t % 2
        self.z, self.xh = self.s // 2, self.s % 2
        self.p = self.c * 16 + self.s
        c, t, s = self.c, self.t, self.s
        self.yp = (c, self.slot(1, 0), s)
        self.ym = (c, self.slot(3, 0), s)
        self.xp = (c, self.slot(0, 1), s)
        self.zp = (c, t, ((self.z + 1) % 8) * 2 + self.xh)
        self.zm = (c, t, ((self.z + 7) % 8) * 2 + self.xh)
        self.x2 = (c, t, self.z * 2 + 1 - self.xh)
        self.xo = (c, self.slot(0, 1), self.z * 2 + 1 - self.xh)
        self.core = (1 - c, t, s)
        before, after = (self.p + PLACES - 1) % PLACES, (self.p + 1) % PLACES
        self.before = (before // 16, before % 16)
        self.after = (after // 16, after % 16)

    def slot(self, dy, other):
        xl = 1 - self.xl if other else self.xl
        return ((self.y + dy) % 4) * 2 + xl

    def tp_peer(self, i):
        return (self.t + i) % TP

    def any_copy(self, dy, other):
        return (self.c, self.slot(dy, other), self.z * 2 + (1 - self.xh if other else self.xh))

    def at_tp(self, t):
        return (self.c, t, self.s)

    def last_before(self):
        return (self.before[0], TP - 1, self.before[1])

    def at_after(self, t):
        return (self.after[0], t, self.after[1])


class Gather:
    def __init__(self, here, region, own, send, recv, arrived, xp):
        self.here, self.region, self.own, self.xp = here, region, own, xp
        self.send_sem, self.recv_sem, self.arrived = send, recv, arrived
        self.sent = []

    def send(self, m, to, slot, part, half=None, own=False):
        src = self.own(part) if own else self.region(slot, part, half)
        copy = remote(src, self.region(slot, part, half), self.send_sem.at[m], self.recv_sem.at[m], to)
        copy.start()
        self.sent.append(copy)

    def wait(self, m, slot, part, half=None):
        ref = self.region(slot, part, half)
        remote(ref, ref, self.send_sem.at[m], self.recv_sem.at[m], self.xp).wait_recv()

    def begin(self, part):
        if part == 0:
            self.begin_x(0)
            self.begin_y(0)
        else:
            self.begin_y(1)
            self.begin_x(1)

    def begin_x(self, part):
        self.send(3 * part, self.xp, self.here.t, part, own=True)

    def begin_y(self, part):
        h = self.here
        self.send(3 * part + 1, h.yp, h.t, part, own=True)
        self.send(3 * part + 2, h.ym, h.t, part, own=True)

    def steps(self):
        h = self.here
        slot = h.slot
        self.wait(0, slot(0, 1), 0)
        self.send(6, h.yp, slot(0, 1), 0)
        self.send(7, h.ym, slot(0, 1), 0)
        self.arrived(slot(0, 1), 0, 0)
        yield
        self.wait(4, slot(3, 0), 1)
        self.send(12, self.xp, slot(3, 0), 1)
        self.send(14, h.yp, slot(3, 0), 1, 0)
        self.arrived(slot(3, 0), 1, 1)
        yield
        self.wait(5, slot(1, 0), 1)
        self.send(13, self.xp, slot(1, 0), 1)
        self.send(15, h.ym, slot(1, 0), 1, 1)
        self.arrived(slot(1, 0), 1, 2)
        yield
        self.wait(1, slot(3, 0), 0)
        self.send(8, h.yp, slot(3, 0), 0, 0)
        self.arrived(slot(3, 0), 0, 3)
        yield
        self.wait(2, slot(1, 0), 0)
        self.send(9, h.ym, slot(1, 0), 0, 1)
        self.arrived(slot(1, 0), 0, 4)
        yield
        self.wait(3, slot(0, 1), 1)
        self.arrived(slot(0, 1), 1, 5)
        yield
        self.wait(14, slot(2, 0), 1, 0)
        self.send(16, self.xp, slot(2, 0), 1, 0)
        self.wait(15, slot(2, 0), 1, 1)
        self.send(17, self.xp, slot(2, 0), 1, 1)
        self.arrived(slot(2, 0), 1, 6)
        yield
        self.wait(6, slot(3, 1), 0)
        self.send(10, h.yp, slot(3, 1), 0, 0)
        self.arrived(slot(3, 1), 0, 7)
        yield
        self.wait(7, slot(1, 1), 0)
        self.send(11, h.ym, slot(1, 1), 0, 1)
        self.arrived(slot(1, 1), 0, 8)
        yield
        self.wait(8, slot(2, 0), 0, 0)
        self.wait(9, slot(2, 0), 0, 1)
        self.arrived(slot(2, 0), 0, 9)
        yield
        self.wait(12, slot(3, 1), 1)
        self.arrived(slot(3, 1), 1, 10)
        yield
        self.wait(13, slot(1, 1), 1)
        self.arrived(slot(1, 1), 1, 11)
        yield
        self.wait(10, slot(2, 1), 0, 0)
        self.wait(11, slot(2, 1), 0, 1)
        self.arrived(slot(2, 1), 0, 12)
        yield
        self.wait(16, slot(2, 1), 1, 0)
        self.wait(17, slot(2, 1), 1, 1)
        self.arrived(slot(2, 1), 1, 13)

    def order(self):
        s = self.here.slot
        return [
            (s(0, 1), 0), (s(3, 0), 1), (s(1, 0), 1), (s(3, 0), 0), (s(1, 0), 0), (s(0, 1), 1), (s(2, 0), 1),
            (s(3, 1), 0), (s(1, 1), 0), (s(2, 0), 0), (s(3, 1), 1), (s(1, 1), 1), (s(2, 1), 0), (s(2, 1), 1),
        ]

    def finish(self):
        for copy in self.sent:
            copy.wait_send()


class Ring:
    OFFSET = [0, 7, 1, 6, 2, 5, 3, 4]

    def __init__(self, here, region, sems, flip):
        self.here, self.region, self.flip = here, region, flip
        self.send_sem, self.recv_sem, self.core_send, self.core_recv = sems
        self.sent = []

    def push(self, way, r):
        h = self.here
        z = (h.z + (8 - r if way == 0 else r)) % 8
        ref = self.region(z, h.c)
        m = way * 4 + r
        copy = remote(ref, ref, self.send_sem.at[m], self.recv_sem.at[m], h.zp if way == 0 else h.zm)
        copy.start()
        self.sent.append(copy)

    def share(self, k):
        h = self.here
        ref = self.region((h.z + self.dz(k)) % 8, h.c)
        copy = remote(ref, ref, self.core_send.at[k], self.core_recv.at[k], h.core)
        copy.start()
        self.sent.append(copy)

    def dz(self, k):
        return self.OFFSET[k] if not self.flip else (8 - self.OFFSET[k]) % 8

    def wait(self, way, r, k):
        h = self.here
        ref = self.region((h.z + self.dz(k)) % 8, h.c)
        m = way * 4 + r
        remote(ref, ref, self.send_sem.at[m], self.recv_sem.at[m], h.zp).wait_recv()

    def steps(self):
        first, second = (1, 0) if self.flip else (0, 1)
        self.push(first, 0)
        self.push(second, 0)
        self.share(0)
        yield
        for r in range(3):
            self.wait(first, r, 1 + 2 * r)
            self.push(first, r + 1)
            self.share(1 + 2 * r)
            self.wait(second, r, 2 + 2 * r)
            if r < 2:
                self.push(second, r + 1)
            self.share(2 + 2 * r)
            yield
        self.wait(first, 3, 7)
        self.share(7)
        yield

    def collect(self):
        h = self.here
        for k in range(8):
            ref = self.region((h.z + self.dz(k)) % 8, 1 - h.c)
            remote(ref, ref, self.core_send.at[k], self.core_recv.at[k], h.core).wait_recv()

    def finish(self):
        for copy in self.sent:
            copy.wait_send()


def advance(steps, n=1):
    for _ in range(n):
        next(steps, None)


def kernel(
    hidden, gain, trace, counts, offsets, w_skv, w_eq, w_eo, w_cq, w_ckv, w_co, out,
    hid, wproj, acc, ssq, kv_s, q_s, tr, picked, rows, enc_w, wck, woc, kvx, qx, qh, eq, ea, enc,
    att_own, attg, tail, attb,
    local, h_send, h_recv, k_send, k_recv, a_send, a_recv, kc_send, kc_recv,
    x_send, x_recv, r_ss, r_rs, r_cs, r_cr,
    p_send, p_recv, halo_send, halo_recv, tail_send, tail_recv,
):
    h = Here()
    c, t, s, z, xh, p = h.c, h.t, h.s, h.z, h.xh, h.p
    is_last = t == TP - 1

    barrier = pltpu.get_barrier_semaphore()
    greet = [h.at_tp(h.tp_peer(i)) for i in range(1, TP)]
    greet += [h.any_copy(dy, 1) for dy in range(4)]
    greet += [h.zp, h.zm, h.x2, h.core, h.last_before()]
    for device in greet:
        pl.semaphore_signal(barrier, inc=1, device_id=device, device_id_type=MESH)

    @pl.when(is_last)
    def _():
        for other in range(TP):
            pl.semaphore_signal(barrier, inc=1, device_id=h.at_after(other), device_id_type=MESH)

    pl.semaphore_wait(barrier, len(greet) + TP * (t // (TP - 1)))

    pushes = []

    def push(src, dst, send, recv, to):
        copy = remote(src, dst, send, recv, to)
        copy.start()
        pushes.append(copy)

    def came(ref, recv):
        remote(ref, ref, p_send.at[0, 0], recv, h.core).wait_recv()

    def bring(src, dst, i):
        copy = pltpu.make_async_copy(src, dst, local.at[i])
        copy.start()
        return copy

    def project(slot, part, index):
        here = pl.ds(part * 256, 256)
        wide = hid[slot, here, :].astype(F32)
        squares = jnp.sum(wide * wide, axis=-1, keepdims=True)
        scaled = (wide * gain[slot]).astype(BF)
        w = wproj[pl.ds(pl.multiple_of(slot * 512, 512), 512), :]
        product = dot(scaled, w)
        if index is None:
            ssq[here, :] = squares
            acc[here, :] = product
        else:
            ssq[here, :] += squares
            acc[here, :] += product

    def hid_gather(i):
        def region(slot, part, half):
            base = part * 256 + i * 128
            if half is None:
                return hid.at[slot, pl.ds(base, 128)]
            return hid.at[slot, pl.ds(base + half * 64, 64)]

        def own(part):
            return hidden.at[pl.ds(part * 256 + i * 128, 128)]

        def arrived(slot, part, index):
            if i == 1:
                project(slot, part, index)

        return Gather(h, region, own, h_send.at[i], h_recv.at[i], arrived, h.xp)

    gather_h = [hid_gather(0), hid_gather(1)]
    for g in gather_h:
        g.begin(0)
        g.begin(1)
    steps_h = [g.steps() for g in gather_h]

    mine = pl.ds(p * 8, 8)
    halves = pl.ds(c * 32, 32)
    push(trace, tr.at[mine], x_send.at[0], x_recv.at[0], h.x2)
    own_trace = bring(trace, tr.at[mine], 0)
    own_hid = bring(hidden, hid.at[t], 1)
    own_skv = bring(w_skv, wproj.at[:, pl.ds(0, 256)], 2)
    own_cq = bring(w_cq, wproj.at[:, pl.ds(256, 256)], 3)
    own_eq = bring(w_eq.at[halves], enc_w.at[0, s, c], 4)
    own_eo = bring(w_eo.at[halves], enc_w.at[1, s, c], 5)
    own_ckv = [bring(w_ckv.at[pl.ds(512 * i, 256)], wck.at[t, pl.ds(512 * i, 256)], 6 + i) for i in range(2)]
    ck_rows = pl.ds(c * 512 + 256 + z * 32, 32)
    own_ckv.append(bring(w_ckv.at[ck_rows], wck.at[t, ck_rows], 8))
    co_rows = pl.ds(z * 32 + c * 16, 16)
    own_co = bring(w_co.at[co_rows, pl.ds(pl.multiple_of(t * 512, 512), 512)], woc.at[t, z * 2 + c], 9)

    def ring(i, region, flip):
        return Ring(h, region, (r_ss.at[i], r_rs.at[i], r_cs.at[i], r_cr.at[i]), flip)

    def trace_ring(i, sel):
        return ring(i, lambda zz, cc: tr.at[pl.ds((cc * 16 + zz * 2 + sel) * 8, 8)], bool(i % 2))

    def enc_ring(i, sel):
        return ring(i, lambda zz, cc: enc_w.at[:, zz * 2 + sel, cc], bool(i % 2))

    def ckv_ring(i):
        return ring(
            i, lambda zz, cc: wck.at[pl.ds(4 * (i % 2), 4), pl.ds(cc * 512 + 256 + zz * 32, 32)], bool(i % 2)
        )

    def co_ring(i):
        return ring(i, lambda zz, cc: woc.at[pl.ds(4 * (i % 2), 4), zz * 2 + cc], bool(i % 2))

    rings_t = [trace_ring(0, xh), trace_ring(1, 1 - xh)]
    rings_e = [enc_ring(2, xh), enc_ring(3, 1 - xh)]
    rings_k = [ckv_ring(4), ckv_ring(5)]
    rings_o = [co_ring(6), co_ring(7)]
    rings = rings_t + rings_e + rings_k + rings_o
    steps_t, steps_e, steps_k2, steps_o = (
        [r.steps() for r in group] for group in (rings_t, rings_e, rings_k, rings_o)
    )

    own_trace.wait()
    advance(steps_t[0])
    came(tr.at[pl.ds((p + 1 - 2 * xh) * 8, 8)], x_recv.at[0])
    advance(steps_t[1])

    def wck_region(slot, part, half):
        base = c * 512 + part * 128
        if half is None:
            return wck.at[slot, pl.ds(base, 128)]
        return wck.at[slot, pl.ds(base + half * 64, 64)]

    def share(slot, part, index):
        ref = wck_region(slot, part, None)
        push(ref, ref, kc_send.at[index], kc_recv.at[index], h.core)

    gather_k = Gather(
        h, wck_region, lambda part: w_ckv.at[pl.ds(c * 512 + part * 128, 128)], k_send, k_recv, share, h.xo
    )
    gather_k.begin_x(0)
    gather_k.begin_x(1)
    steps_k = gather_k.steps()

    others = [(0, 1), (1, 0), (3, 0), (1, 1), (3, 1), (2, 0), (2, 1)]
    for i, (dy, other) in enumerate(others):
        push(w_ckv.at[ck_rows], wck.at[t, ck_rows], p_send.at[0, i], p_recv.at[0, i], h.any_copy(dy, other))
    push(w_eq.at[halves], enc_w.at[0, s, c], x_send.at[1], x_recv.at[1], h.x2)
    push(w_eo.at[halves], enc_w.at[1, s, c], x_send.at[2], x_recv.at[2], h.x2)
    for i, (dy, other) in enumerate(others):
        cols = pl.ds(pl.multiple_of(h.slot(dy, other) * 512, 512), 512)
        push(
            w_co.at[co_rows, cols], woc.at[t, z * 2 + c], p_send.at[1, i], p_recv.at[1, i],
            h.any_copy(dy, other),
        )

    own_hid.wait()
    own_skv.wait()
    own_cq.wait()
    project(t, 0, None)
    project(t, 1, None)

    def both(steps, n=1):
        for _ in range(n):
            for one in steps:
                advance(one)

    both(steps_h, 2)
    both(steps_t)
    both(steps_h, 3)
    both(steps_t)
    own_eq.wait()
    own_eo.wait()
    advance(steps_e[0])
    both(steps_h, 3)
    both(steps_t)
    for w in range(2):
        came(enc_w.at[w, z * 2 + 1 - xh, c], x_recv.at[1 + w])
    advance(steps_e[1])
    both(steps_h, 2)
    both(steps_t)

    for r in rings_t:
        r.collect()

    def pick(owner):
        for k in range(4):
            at = p * 8 + owner - offsets[owner, k]
            at = jnp.minimum(jnp.maximum(at, 0), 254)
            picked[owner, 128 * k : 128 * k + 64, :] = tr[at]
            picked[owner, 128 * k + 64 : 128 * k + 128, :] = tr[at + 1]

    columns = pl.ds(pl.multiple_of(t * 128, 128), 128)
    for i in range(1, TP):
        to = h.tp_peer(i)
        pick(to)
        push(picked.at[to], rows.at[:, columns], p_send.at[3, i], p_recv.at[3, i], h.at_tp(to))
    pick(t)
    rows[:, columns] = picked[t]

    both(steps_h, 2)
    both(steps_e)
    both(steps_h, 2)

    inverse = lax.rsqrt(ssq[...] * (1.0 / 4096) + EPS)
    projected = (acc[...] * inverse).astype(BF)
    kv_s[...] = projected[:, :256]
    q_s[0:512, :] = projected[:, 256:]
    q_s[512:576, :] = jnp.zeros((64, 256), BF)
    for i in range(1, TP):
        to = h.tp_peer(i)
        mine_there = pl.ds(pl.multiple_of(to * 64, 64), 64)
        push(kv_s.at[mine_there], kvx.at[t], p_send.at[2, i], p_recv.at[2, i], h.at_tp(to))
    kvx[t] = kv_s[pl.ds(pl.multiple_of(t * 64, 64), 64), :]

    for i in range(1, TP):
        to = h.tp_peer(i)
        mine_there = pl.ds(pl.multiple_of(to * 64 + 48, 16), 80)
        push(q_s.at[mine_there], qx.at[t], p_send.at[4, i], p_recv.at[4, i], h.at_tp(to))
    qx[t] = q_s[pl.ds(pl.multiple_of(t * 64 + 48, 16), 80), :]
    push(q_s.at[pl.ds(0, 64)], qh.at[t], halo_send.at[0], halo_recv.at[t], h.last_before())

    both(steps_e)
    for copy in own_ckv:
        copy.wait()
    for i, (dy, other) in enumerate(others):
        came(wck.at[h.slot(4 - dy, other), ck_rows], p_recv.at[0, i])
    both(steps_e)
    both(steps_k2)
    own_co.wait()
    for i, (dy, other) in enumerate(others):
        came(woc.at[h.slot(4 - dy, other), z * 2 + c], p_recv.at[1, i])

    def from_peer(i):
        return h.tp_peer(TP - i)

    for i in range(1, TP):
        cols = pl.ds(pl.multiple_of(from_peer(i) * 128, 128), 128)
        came(rows.at[:, cols], p_recv.at[3, i])
    gather_k.begin_y(1)
    gather_k.begin_y(0)
    advance(steps_k, 1)
    both(steps_e)
    both(steps_k2)
    for r in rings_e:
        r.collect()
    for n in range(4):
        cols = slice(256 * n, 256 * (n + 1))
        eq[:, cols] = dot(rows[...], enc_w[0, :, :, :, cols].reshape(1024, 256)).astype(BF)
    advance(steps_k, 2)
    both(steps_k2)
    for i in range(1, TP):
        came(kvx.at[from_peer(i)], p_recv.at[2, i])
    advance(steps_k, 2)
    for e in range(8):
        cols = slice(128 * e, 128 * (e + 1))
        scores = dot_t(eq[:, cols], kvx[e, :, :128]) * FACTOR
        top = jnp.max(scores, axis=-1, keepdims=True)
        weights = jnp.exp(scores - top)
        probs = (weights / jnp.sum(weights, axis=-1, keepdims=True)).astype(BF)
        ea[:, cols] = dot(probs, kvx[e, :, 128:]).astype(BF)
        advance(steps_k, 1)
        if e == 3:
            both(steps_k2)
            both(steps_o)
    for n in range(4):
        cols = slice(256 * n, 256 * (n + 1))
        update = dot(ea[...], enc_w[1, :, :, :, cols].reshape(1024, 256))
        enc[:, cols] = (rows[:, cols].astype(F32) + update).astype(BF)
        advance(steps_k, 1)
    both(steps_k2)
    both(steps_o)

    for i in range(1, TP):
        came(qx.at[from_peer(i)], p_recv.at[4, i])

    @pl.when(is_last)
    def _():
        for j in range(TP):
            came(qh.at[j], halo_recv.at[j])
            qx[j, 16:80, :] = qh[j]

    for index, (slot, part) in enumerate(gather_k.order()):
        came(wck.at[slot, pl.ds((1 - c) * 512 + part * 128, 128)], kc_recv.at[index])
    for r in rings_k:
        r.collect()

    live_keys = counts[t] * 128
    lane = lax.broadcasted_iota(jnp.int32, (80, 512), 1)
    mask = lane < live_keys
    row = lax.broadcasted_iota(jnp.int32, (80, 128), 0)
    keep = (row >= 15) & (row < 79)

    def att_gather(i):
        def region(slot, part, half):
            base = i * 1024 + part * 512
            if half is None:
                return attg.at[slot, :, pl.ds(base, 512)]
            return attg.at[slot, :, pl.ds(base + half * 256, 256)]

        def own(part):
            return att_own.at[:, pl.ds(i * 1024 + part * 512, 512)]

        return Gather(h, region, own, a_send.at[i], a_recv.at[i], lambda *_: None, h.xp)

    gather_a = [att_gather(0), att_gather(1)]
    steps_a = [g.steps() for g in gather_a]

    def tail_copy(j):
        return remote(
            att_own.at[pl.ds(16, 64), pl.ds(256 * j, 256)], tail.at[j],
            tail_send.at[j], tail_recv.at[0], h.at_after(j),
        )

    for j in range(TP):
        pair = dot(enc[...], wck[j]).astype(BF)
        for half in range(2):
            key = pair[:, 256 * half : 256 * half + 128]
            value = pair[:, 256 * half + 128 : 256 * half + 256]
            query = qx[j, :, 128 * half : 128 * half + 128]
            scores = jnp.where(mask, dot_t(query, key) * FACTOR, NEG)
            top = jnp.max(scores, axis=-1, keepdims=True)
            weights = jnp.where(mask, jnp.exp(scores - top), 0.0)
            total = jnp.sum(weights, axis=-1, keepdims=True)
            total = jnp.where(total > 0.0, total, 1.0)
            probs = (weights / total).astype(BF)
            mixed = jnp.where(keep, dot(probs, value), 0.0).astype(BF)
            at = 256 * j + 128 * half
            att_own[:, at : at + 128] = mixed

        @pl.when(is_last)
        def _():
            tail_copy(j).start()

        if j == 1:
            gather_a[0].begin(0)
        if j == 3:
            gather_a[0].begin(1)
            both(steps_o)
        if j == 4:
            advance(steps_a[0], 1)
        if j == 5:
            gather_a[1].begin(0)
            both(steps_o)
        if j == 6:
            advance(steps_a[0], 3)
    gather_a[1].begin(1)
    both(steps_o)
    advance(steps_a[0], 2)
    came(tail.at[t], tail_recv.at[0])
    for i in range(1, TP):
        push(tail.at[t], tail.at[t], p_send.at[5, i], p_recv.at[5, i], h.at_tp(h.tp_peer(i)))
    advance(steps_a[0], 1)
    advance(steps_a[1], 2)
    advance(steps_a[0], 2)
    advance(steps_a[1], 2)
    advance(steps_a[0], 3)
    advance(steps_a[1], 3)
    advance(steps_a[0], 2)
    attg[t] = att_own[...]
    for i in range(1, TP):
        came(tail.at[from_peer(i)], p_recv.at[5, i])
    for r in rings_o:
        r.collect()

    def attended(i):
        cols = slice(1024 * i, 1024 * (i + 1))
        for j in range(4 * i, 4 * i + 4):
            attb[0:64, 256 * j : 256 * (j + 1)] = jnp.where(p > 0, tail[j].astype(F32), 0.0).astype(BF)
        for v in range(TP):
            if v:
                attb[64 * v : 64 * v + 64, cols] = attg[v - 1, 16:80, cols]
            attb[64 * v + 48 : 64 * v + 64, cols] += attg[v, 0:16, cols]
        return dot(attb[:, cols], woc[4 * i : 4 * i + 4].reshape(1024, 512))

    acc[...] = hid[t].astype(F32) + attended(0)
    advance(steps_a[1], 7)
    out[...] = (acc[...] + attended(1)).astype(BF)

    for group in gather_h + [gather_k] + gather_a + rings:
        group.finish()
    for copy in pushes:
        copy.wait_send()

    @pl.when(is_last)
    def _():
        for j in range(TP):
            tail_copy(j).wait_send()


def body(hidden, gain, trace, counts, offsets, w_skv, w_eq, w_eo, w_cq, w_ckv, w_co):
    any_ = pl.BlockSpec(memory_space=pl.ANY)
    vmem = pl.BlockSpec(memory_space=pltpu.VMEM)
    smem = pl.BlockSpec(memory_space=pltpu.SMEM)
    dma = pltpu.SemaphoreType.DMA
    v = pltpu.VMEM
    scratch = [
        v((8, 512, 512), BF),
        v((4096, 512), BF),
        v((512, 512), F32),
        v((512, 1), F32),
        v((512, 256), BF),
        v((576, 256), BF),
        v((256, 64, 128), BF),
        v((8, 512, 128), BF),
        v((512, 1024), BF),
        v((2, 16, 2, 32, 1024), BF),
        v((8, 1024, 512), BF),
        v((8, 16, 16, 512), BF),
        v((8, 64, 256), BF),
        v((8, 80, 256), BF),
        v((8, 64, 256), BF),
        v((512, 1024), BF),
        v((512, 1024), BF),
        v((512, 1024), BF),
        v((80, 2048), BF),
        v((8, 80, 2048), BF),
        v((8, 64, 256), BF),
        v((512, 2048), BF),
        dma((10,)),
        dma((2, 18)), dma((2, 18)), dma((18,)), dma((18,)), dma((2, 18)), dma((2, 18)), dma((14,)), dma((14,)),
        dma((3,)), dma((3,)),
        dma((8, 8)), dma((8, 8)), dma((8, 8)), dma((8, 8)),
        dma((6, 8)), dma((6, 8)),
        dma((1,)), dma((8,)), dma((8,)), dma((1,)),
    ]
    return pl.pallas_call(
        kernel,
        out_shape=jax.ShapeDtypeStruct((512, 512), BF),
        in_specs=[any_, vmem, any_, smem, smem, any_, any_, any_, any_, any_, any_],
        out_specs=vmem,
        scratch_shapes=scratch,
        compiler_params=pltpu.CompilerParams(
            collective_id=0, has_side_effects=True, vmem_limit_bytes=58 << 20
        ),
        cost_estimate=pl.CostEstimate(flops=11_000_000_000, bytes_accessed=14_000_000, transcendentals=1_000_000),
    )(
        hidden, gain.astype(F32).reshape(8, 1, 512), trace.reshape(8, 64, 128), counts, offsets,
        w_skv, w_eq, w_eo, w_cq, w_ckv, w_co,
    )


def solution(mesh):
    place = ("seq", "section")
    in_specs = (
        P(place, "tp"), P(), P(place, "tp"), P(place), P(place, None), P(None, "tp"),
        P("section", None), P("section", None), P(None, "tp"), P(None, "tp"), P("tp", None),
    )
    return jax.shard_map(body, mesh=mesh, in_specs=in_specs, out_specs=P(place, "tp"), check_vma=False)
```

time: 154 us -> 137 us (0.89)
  Pallas kernels: 149 us -> 132 us
    pallas_call x1, Pallas kernels: 149 us -> 132 us  [body(): pl.pallas_call(kernel, out_shape=jax.ShapeDtypeStruct((512, 512), BF), in...]
where the time goes in v2:
time: 137 us
  Pallas kernels  132 us (96%)
  local copies, waits for them, and re-layouts  3.22 us (2%)
    pallas_call x1, Pallas kernels, body(): pl.pallas_call(kernel, out_shape=jax.ShapeDtypeStruct((512, 512), BF), in...  132 us
    unnamed x2, local copies, waits for them, and re-layouts  3.22 us

profile of v2, /device:TPU:1, one launch (start us, length us, event | category | flops | bytes accessed | tf_op | source)
XLA Modules:
  0.0 137.0 jit_solution(8999398019070994214)
XLA Ops:
  0.0 1.3 copy.12.offsets
  1.3 1.3 reshape.11
  2.7 132.4 %shard_map.109 = bf16[512,512]{1,0:T(8,128)(2,1)} custom-call(bf16[512,512]{1,0:T(8,128)(2,1)} %hidden.1, f32[8,1,512]{2,1,0:T(1,128)} %bitcast.2, bf16[8,64,128]{2,1,0:T(8,128)(2,1)} %bitcast.3, s32[8]{0:T(128)} %counts.1, s32[8,4]{1,0:T(8,128)} %copy.12.offsets, bf16[4096,256]{1,0:T(8,128)(2,1)} %w_skv.1, bf16[64,1024]{1,0:T(8,128)(2,1)} %w_eq.1, ...), custom_call_target="tpu_custom_call" | custom-call | flops 11000000512 | bytes 14000000 | tf_op jit(solution)/shard_map/pallas_call | solution.py:671
  135.1 1.9 %copy.14 = bf16[512,512]{1,0:T(8,128)(2,1)} copy(bf16[512,512]{1,0:T(8,128)(2,1)} %shard_map.109) | data formatting | bytes 1048576

commit v3 on v2

--- a/solution.py
+++ b/solution.py
@@ -247,8 +247,8 @@
 
 
 def kernel(
-    hidden, gain, trace, counts, offsets, w_skv, w_eq, w_eo, w_cq, w_ckv, w_co, out,
-    hid, wproj, acc, ssq, kv_s, q_s, tr, picked, rows, enc_w, wck, woc, kvx, qx, qh, eq, ea, enc,
+    hidden, gain_in, trace, counts, offsets, w_skv, w_eq, w_eo, w_cq, w_ckv, w_co, out,
+    gain, hid, wproj, acc, ssq, kv_s, q_s, tr, picked, rows, enc_w, wck, woc, kvx, qx, qh, eq, ea, enc,
     att_own, attg, tail, attb,
     local, h_send, h_recv, k_send, k_recv, a_send, a_recv, kc_send, kc_recv,
     x_send, x_recv, r_ss, r_rs, r_cs, r_cr,
@@ -398,6 +398,8 @@
             h.any_copy(dy, other),
         )
 
+    for i in range(TP):
+        gain[i] = gain_in[512 * i : 512 * (i + 1)].astype(F32).reshape(1, 512)
     own_hid.wait()
     own_skv.wait()
     own_cq.wait()
@@ -429,7 +431,7 @@
 
     def pick(owner):
         for k in range(4):
-            at = p * 8 + owner - offsets[owner, k]
+            at = p * 8 + owner - offsets[k, owner]
             at = jnp.minimum(jnp.maximum(at, 0), 254)
             picked[owner, 128 * k : 128 * k + 64, :] = tr[at]
             picked[owner, 128 * k + 64 : 128 * k + 128, :] = tr[at + 1]
@@ -501,7 +503,7 @@
         scores = dot_t(eq[:, cols], kvx[e, :, :128]) * FACTOR
         top = jnp.max(scores, axis=-1, keepdims=True)
         weights = jnp.exp(scores - top)
-        probs = (weights / jnp.sum(weights, axis=-1, keepdims=True)).astype(BF)
+        probs = (weights * (1.0 / jnp.sum(weights, axis=-1, keepdims=True))).astype(BF)
         ea[:, cols] = dot(probs, kvx[e, :, 128:]).astype(BF)
         advance(steps_k, 1)
         if e == 3:
@@ -530,10 +532,9 @@
         r.collect()
 
     live_keys = counts[t] * 128
-    lane = lax.broadcasted_iota(jnp.int32, (80, 512), 1)
-    mask = lane < live_keys
-    row = lax.broadcasted_iota(jnp.int32, (80, 128), 0)
-    keep = (row >= 15) & (row < 79)
+    mask = lax.broadcasted_iota(jnp.int32, (160, 512), 1) < live_keys
+    any_live = jnp.zeros((64, 128), jnp.int32) + live_keys > 0
+    last_row = lax.broadcasted_iota(jnp.int32, (64, 128), 0) == 63
 
     def att_gather(i):
         def region(slot, part, half):
@@ -552,25 +553,23 @@
 
     def tail_copy(j):
         return remote(
-            att_own.at[pl.ds(16, 64), pl.ds(256 * j, 256)], tail.at[j],
+            att_own.at[:, pl.ds(256 * j, 256)], tail.at[j],
             tail_send.at[j], tail_recv.at[0], h.at_after(j),
         )
 
     for j in range(TP):
         pair = dot(enc[...], wck[j]).astype(BF)
-        for half in range(2):
-            key = pair[:, 256 * half : 256 * half + 128]
-            value = pair[:, 256 * half + 128 : 256 * half + 256]
-            query = qx[j, :, 128 * half : 128 * half + 128]
-            scores = jnp.where(mask, dot_t(query, key) * FACTOR, NEG)
-            top = jnp.max(scores, axis=-1, keepdims=True)
-            weights = jnp.where(mask, jnp.exp(scores - top), 0.0)
-            total = jnp.sum(weights, axis=-1, keepdims=True)
-            total = jnp.where(total > 0.0, total, 1.0)
-            probs = (weights / total).astype(BF)
-            mixed = jnp.where(keep, dot(probs, value), 0.0).astype(BF)
-            at = 256 * j + 128 * half
-            att_own[:, at : at + 128] = mixed
+        scores = jnp.concatenate(
+            [dot_t(qx[j, :, 128 * i : 128 * i + 128], pair[:, 256 * i : 256 * i + 128]) for i in range(2)], axis=0
+        )
+        scores = jnp.where(mask, scores * FACTOR, NEG)
+        weights = jnp.exp(scores - jnp.max(scores, axis=-1, keepdims=True))
+        probs = (weights * (1.0 / jnp.sum(weights, axis=-1, keepdims=True))).astype(BF)
+        for i in range(2):
+            mixed = dot(probs[80 * i : 80 * i + 80], pair[:, 256 * i + 128 : 256 * i + 256])
+            mixed = jnp.where(last_row, mixed[15:16], mixed[16:80])
+            at = 256 * j + 128 * i
+            att_own[:, at : at + 128] = jnp.where(any_live, mixed, 0.0).astype(BF)
 
         @pl.when(is_last)
         def _():
@@ -607,14 +606,18 @@
     for r in rings_o:
         r.collect()
 
+    own_row = lax.broadcasted_iota(jnp.int32, (16, 1024), 0) == 15
+
     def attended(i):
         cols = slice(1024 * i, 1024 * (i + 1))
         for j in range(4 * i, 4 * i + 4):
             attb[0:64, 256 * j : 256 * (j + 1)] = jnp.where(p > 0, tail[j].astype(F32), 0.0).astype(BF)
         for v in range(TP):
             if v:
-                attb[64 * v : 64 * v + 64, cols] = attg[v - 1, 16:80, cols]
-            attb[64 * v + 48 : 64 * v + 64, cols] += attg[v, 0:16, cols]
+                attb[64 * v : 64 * v + 64, cols] = attg[v - 1, :, cols]
+            attb[64 * v + 48 : 64 * v + 64, cols] = jnp.where(
+                own_row, attg[v, 48:64, cols], attb[64 * v + 48 : 64 * v + 64, cols]
+            )
         return dot(attb[:, cols], woc[4 * i : 4 * i + 4].reshape(1024, 512))
 
     acc[...] = hid[t].astype(F32) + attended(0)
@@ -639,6 +642,7 @@
     dma = pltpu.SemaphoreType.DMA
     v = pltpu.VMEM
     scratch = [
+        v((8, 1, 512), F32),
         v((8, 512, 512), BF),
         v((4096, 512), BF),
         v((512, 512), F32),
@@ -657,8 +661,8 @@
         v((512, 1024), BF),
         v((512, 1024), BF),
         v((512, 1024), BF),
-        v((80, 2048), BF),
-        v((8, 80, 2048), BF),
+        v((64, 2048), BF),
+        v((8, 64, 2048), BF),
         v((8, 64, 256), BF),
         v((512, 2048), BF),
         dma((10,)),
@@ -679,7 +683,7 @@
         ),
         cost_estimate=pl.CostEstimate(flops=11_000_000_000, bytes_accessed=14_000_000, transcendentals=1_000_000),
     )(
-        hidden, gain.astype(F32).reshape(8, 1, 512), trace.reshape(8, 64, 128), counts, offsets,
+        hidden, gain, trace.reshape(8, 64, 128), counts, offsets.T,
         w_skv, w_eq, w_eo, w_cq, w_ckv, w_co,
     )
 

time: 137 us -> 132 us (0.964)
  Pallas kernels: 132 us -> 130 us
    pallas_call x1, Pallas kernels: 132 us -> 130 us  [body(): pl.pallas_call(kernel, out_shape=jax.ShapeDtypeStruct((512, 512), BF), in...]
    unnamed x2 -> x1, local copies, waits for them, and re-layouts: 3.22 us -> 1.87 us
where the time goes in v3:
time: 132 us
  Pallas kernels  130 us (98%)
  local copies, waits for them, and re-layouts  1.87 us (1%)
    pallas_call x1, Pallas kernels, body(): pl.pallas_call(kernel, out_shape=jax.ShapeDtypeStruct((512, 512), BF), in...  130 us

profile of v3, /device:TPU:1, one launch (start us, length us, event | category | flops | bytes accessed | tf_op | source)
XLA Modules:
  0.0 132.0 jit_solution(3042592696081423164)
XLA Ops:
  0.0 130.2 %shard_map.109 = bf16[512,512]{1,0:T(8,128)(2,1)} custom-call(bf16[512,512]{1,0:T(8,128)(2,1)} %hidden.1, bf16[4096]{0:T(1024)(128)(2,1)} %gain_in.1, bf16[8,64,128]{2,1,0:T(8,128)(2,1)} %bitcast.2, s32[8]{0:T(128)} %counts.1, s32[4,8]{1,0:T(4,128)} %bitcast.3, bf16[4096,256]{1,0:T(8,128)(2,1)} %w_skv.1, bf16[64,1024]{1,0:T(8,128)(2,1)} %w_eq.1, ...), custom_call_target="tpu_custom_call" | custom-call | flops 11000000512 | bytes 14000000 | tf_op jit(solution)/shard_map/pallas_call | solution.py:675
  130.2 1.9 %copy.13 = bf16[512,512]{1,0:T(8,128)(2,1)} copy(bf16[512,512]{1,0:T(8,128)(2,1)} %shard_map.109) | data formatting | bytes 1048576

commit v4 on v3

--- a/solution.py
+++ b/solution.py
@@ -181,8 +181,8 @@
 class Ring:
     OFFSET = [0, 7, 1, 6, 2, 5, 3, 4]
 
-    def __init__(self, here, region, sems, flip):
-        self.here, self.region, self.flip = here, region, flip
+    def __init__(self, here, region, sems, flip, cross=None):
+        self.here, self.region, self.flip, self.cross = here, region, flip, cross
         self.send_sem, self.recv_sem, self.core_send, self.core_recv = sems
         self.sent = []
 
@@ -201,6 +201,20 @@
         copy = remote(ref, ref, self.core_send.at[k], self.core_recv.at[k], h.core)
         copy.start()
         self.sent.append(copy)
+        if self.cross:
+            copy = remote(ref, ref, self.cross[0].at[k], self.cross[1].at[k], h.xo)
+            copy.start()
+            self.sent.append(copy)
+
+    def swap(self):
+        h = self.here
+        for k in range(8):
+            ref = self.region((h.z + self.dz(k)) % 8, h.c, 1 - h.xh)
+            remote(ref, ref, self.cross[0].at[k], self.cross[1].at[k], h.xo).wait_recv()
+            copy = remote(ref, ref, self.cross[2].at[k], self.cross[3].at[k], h.core)
+            copy.start()
+            self.sent.append(copy)
+            yield
 
     def dz(self, k):
         return self.OFFSET[k] if not self.flip else (8 - self.OFFSET[k]) % 8
@@ -235,6 +249,9 @@
         for k in range(8):
             ref = self.region((h.z + self.dz(k)) % 8, 1 - h.c)
             remote(ref, ref, self.core_send.at[k], self.core_recv.at[k], h.core).wait_recv()
+            if self.cross:
+                ref = self.region((h.z + self.dz(k)) % 8, 1 - h.c, 1 - h.xh)
+                remote(ref, ref, self.cross[2].at[k], self.cross[3].at[k], h.core).wait_recv()
 
     def finish(self):
         for copy in self.sent:
@@ -251,7 +268,7 @@
     gain, hid, wproj, acc, ssq, kv_s, q_s, tr, picked, rows, enc_w, wck, woc, kvx, qx, qh, eq, ea, enc,
     att_own, attg, tail, attb,
     local, h_send, h_recv, k_send, k_recv, a_send, a_recv, kc_send, kc_recv,
-    x_send, x_recv, r_ss, r_rs, r_cs, r_cr,
+    x_send, x_recv, r_ss, r_rs, r_cs, r_cr, s_xs, s_xr, s_cs, s_cr,
     p_send, p_recv, halo_send, halo_recv, tail_send, tail_recv,
 ):
     h = Here()
@@ -344,8 +361,13 @@
     def trace_ring(i, sel):
         return ring(i, lambda zz, cc: tr.at[pl.ds((cc * 16 + zz * 2 + sel) * 8, 8)], bool(i % 2))
 
-    def enc_ring(i, sel):
-        return ring(i, lambda zz, cc: enc_w.at[:, zz * 2 + sel, cc], bool(i % 2))
+    def enc_ring(i):
+        w = i % 2
+        return Ring(
+            h, lambda zz, cc, sel=xh: enc_w.at[w, zz * 2 + sel, cc],
+            (r_ss.at[i], r_rs.at[i], r_cs.at[i], r_cr.at[i]), bool(w),
+            (s_xs.at[w], s_xr.at[w], s_cs.at[w], s_cr.at[w]),
+        )
 
     def ckv_ring(i):
         return ring(
@@ -356,7 +378,7 @@
         return ring(i, lambda zz, cc: woc.at[pl.ds(4 * (i % 2), 4), zz * 2 + cc], bool(i % 2))
 
     rings_t = [trace_ring(0, xh), trace_ring(1, 1 - xh)]
-    rings_e = [enc_ring(2, xh), enc_ring(3, 1 - xh)]
+    rings_e = [enc_ring(2), enc_ring(3)]
     rings_k = [ckv_ring(4), ckv_ring(5)]
     rings_o = [co_ring(6), co_ring(7)]
     rings = rings_t + rings_e + rings_k + rings_o
@@ -389,8 +411,6 @@
     others = [(0, 1), (1, 0), (3, 0), (1, 1), (3, 1), (2, 0), (2, 1)]
     for i, (dy, other) in enumerate(others):
         push(w_ckv.at[ck_rows], wck.at[t, ck_rows], p_send.at[0, i], p_recv.at[0, i], h.any_copy(dy, other))
-    push(w_eq.at[halves], enc_w.at[0, s, c], x_send.at[1], x_recv.at[1], h.x2)
-    push(w_eo.at[halves], enc_w.at[1, s, c], x_send.at[2], x_recv.at[2], h.x2)
     for i, (dy, other) in enumerate(others):
         cols = pl.ds(pl.multiple_of(h.slot(dy, other) * 512, 512), 512)
         push(
@@ -417,12 +437,10 @@
     both(steps_t)
     own_eq.wait()
     own_eo.wait()
-    advance(steps_e[0])
+    both(steps_e)
     both(steps_h, 3)
     both(steps_t)
-    for w in range(2):
-        came(enc_w.at[w, z * 2 + 1 - xh, c], x_recv.at[1 + w])
-    advance(steps_e[1])
+    both(steps_e)
     both(steps_h, 2)
     both(steps_t)
 
@@ -446,6 +464,11 @@
 
     both(steps_h, 2)
     both(steps_e)
+    for copy in own_ckv:
+        copy.wait()
+    for i, (dy, other) in enumerate(others):
+        came(wck.at[h.slot(4 - dy, other), ck_rows], p_recv.at[0, i])
+    both(steps_k2)
     both(steps_h, 2)
 
     inverse = lax.rsqrt(ssq[...] * (1.0 / 4096) + EPS)
@@ -467,11 +490,10 @@
     push(q_s.at[pl.ds(0, 64)], qh.at[t], halo_send.at[0], halo_recv.at[t], h.last_before())
 
     both(steps_e)
-    for copy in own_ckv:
-        copy.wait()
-    for i, (dy, other) in enumerate(others):
-        came(wck.at[h.slot(4 - dy, other), ck_rows], p_recv.at[0, i])
+    swaps = [r.swap() for r in rings_e]
+    both(swaps, 3)
     both(steps_e)
+    both(swaps, 2)
     both(steps_k2)
     own_co.wait()
     for i, (dy, other) in enumerate(others):
@@ -486,7 +508,7 @@
     gather_k.begin_y(1)
     gather_k.begin_y(0)
     advance(steps_k, 1)
-    both(steps_e)
+    both(swaps, 3)
     both(steps_k2)
     for r in rings_e:
         r.collect()
@@ -669,6 +691,7 @@
         dma((2, 18)), dma((2, 18)), dma((18,)), dma((18,)), dma((2, 18)), dma((2, 18)), dma((14,)), dma((14,)),
         dma((3,)), dma((3,)),
         dma((8, 8)), dma((8, 8)), dma((8, 8)), dma((8, 8)),
+        dma((2, 8)), dma((2, 8)), dma((2, 8)), dma((2, 8)),
         dma((6, 8)), dma((6, 8)),
         dma((1,)), dma((8,)), dma((8,)), dma((1,)),
     ]

time: 132 us -> 129 us (0.977)
  Pallas kernels: 130 us -> 127 us
    pallas_call x1, Pallas kernels: 130 us -> 127 us  [body(): pl.pallas_call(kernel, out_shape=jax.ShapeDtypeStruct((512, 512), BF), in...]
where the time goes in v4:
time: 129 us
  Pallas kernels  127 us (98%)
  local copies, waits for them, and re-layouts  1.87 us (1%)
    pallas_call x1, Pallas kernels, body(): pl.pallas_call(kernel, out_shape=jax.ShapeDtypeStruct((512, 512), BF), in...  127 us

profile of v4, /device:TPU:1, one launch (start us, length us, event | category | flops | bytes accessed | tf_op | source)
XLA Modules:
  0.0 129.1 jit_solution(6974297315374318830)
XLA Ops:
  0.0 127.3 %shard_map.109 = bf16[512,512]{1,0:T(8,128)(2,1)} custom-call(bf16[512,512]{1,0:T(8,128)(2,1)} %hidden.1, bf16[4096]{0:T(1024)(128)(2,1)} %gain_in.1, bf16[8,64,128]{2,1,0:T(8,128)(2,1)} %bitcast.2, s32[8]{0:T(128)} %counts.1, s32[4,8]{1,0:T(4,128)} %bitcast.3, bf16[4096,256]{1,0:T(8,128)(2,1)} %w_skv.1, bf16[64,1024]{1,0:T(8,128)(2,1)} %w_eq.1, ...), custom_call_target="tpu_custom_call" | custom-call | flops 11000000512 | bytes 14000000 | tf_op jit(solution)/shard_map/pallas_call | solution.py:698
  127.3 1.9 %copy.13 = bf16[512,512]{1,0:T(8,128)(2,1)} copy(bf16[512,512]{1,0:T(8,128)(2,1)} %shard_map.109) | data formatting | bytes 1048576

commit v5 on v4

--- a/solution.py
+++ b/solution.py
@@ -489,6 +489,8 @@
     qx[t] = q_s[pl.ds(pl.multiple_of(t * 64 + 48, 16), 80), :]
     push(q_s.at[pl.ds(0, 64)], qh.at[t], halo_send.at[0], halo_recv.at[t], h.last_before())
 
+    gather_k.begin_y(1)
+    gather_k.begin_y(0)
     both(steps_e)
     swaps = [r.swap() for r in rings_e]
     both(swaps, 3)
@@ -505,8 +507,6 @@
     for i in range(1, TP):
         cols = pl.ds(pl.multiple_of(from_peer(i) * 128, 128), 128)
         came(rows.at[:, cols], p_recv.at[3, i])
-    gather_k.begin_y(1)
-    gather_k.begin_y(0)
     advance(steps_k, 1)
     both(swaps, 3)
     both(steps_k2)
@@ -602,16 +602,21 @@
         if j == 3:
             gather_a[0].begin(1)
             both(steps_o)
-        if j == 4:
+        if j == 3:
             advance(steps_a[0], 1)
+        if j == 5:
+            advance(steps_a[0], 2)
         if j == 5:
             gather_a[1].begin(0)
             both(steps_o)
         if j == 6:
-            advance(steps_a[0], 3)
+            advance(steps_a[0], 2)
+        if j == 7:
+            advance(steps_a[0], 1)
     gather_a[1].begin(1)
+    advance(steps_a[1], 1)
+    advance(steps_a[0], 1)
     both(steps_o)
-    advance(steps_a[0], 2)
     came(tail.at[t], tail_recv.at[0])
     for i in range(1, TP):
         push(tail.at[t], tail.at[t], p_send.at[5, i], p_recv.at[5, i], h.at_tp(h.tp_peer(i)))

time: 129 us -> 128 us (level)
  no operation moved by 1% of the time
where the time goes in v5:
time: 128 us
  Pallas kernels  126 us (98%)
  local copies, waits for them, and re-layouts  1.87 us (1%)
    pallas_call x1, Pallas kernels, body(): pl.pallas_call(kernel, out_shape=jax.ShapeDtypeStruct((512, 512), BF), in...  126 us

profile of v5, /device:TPU:1, one launch (start us, length us, event | category | flops | bytes accessed | tf_op | source)
XLA Modules:
  0.0 128.0 jit_solution(1601776690124571178)
XLA Ops:
  0.0 126.1 %shard_map.109 = bf16[512,512]{1,0:T(8,128)(2,1)} custom-call(bf16[512,512]{1,0:T(8,128)(2,1)} %hidden.1, bf16[4096]{0:T(1024)(128)(2,1)} %gain_in.1, bf16[8,64,128]{2,1,0:T(8,128)(2,1)} %bitcast.2, s32[8]{0:T(128)} %counts.1, s32[4,8]{1,0:T(4,128)} %bitcast.3, bf16[4096,256]{1,0:T(8,128)(2,1)} %w_skv.1, bf16[64,1024]{1,0:T(8,128)(2,1)} %w_eq.1, ...), custom_call_target="tpu_custom_call" | custom-call | flops 11000000512 | bytes 14000000 | tf_op jit(solution)/shard_map/pallas_call | solution.py:703
  126.2 1.9 %copy.13 = bf16[512,512]{1,0:T(8,128)(2,1)} copy(bf16[512,512]{1,0:T(8,128)(2,1)} %shard_map.109) | data formatting | bytes 1048576

commit v6 on v5

--- a/solution.py
+++ b/solution.py
@@ -617,11 +617,11 @@
     advance(steps_a[1], 1)
     advance(steps_a[0], 1)
     both(steps_o)
+    advance(steps_a[0], 1)
+    advance(steps_a[1], 2)
     came(tail.at[t], tail_recv.at[0])
     for i in range(1, TP):
         push(tail.at[t], tail.at[t], p_send.at[5, i], p_recv.at[5, i], h.at_tp(h.tp_peer(i)))
-    advance(steps_a[0], 1)
-    advance(steps_a[1], 2)
     advance(steps_a[0], 2)
     advance(steps_a[1], 2)
     advance(steps_a[0], 3)

time: 128 us -> 129 us (level); the launches traced: 128 us -> 127 us
    pallas_call x1, Pallas kernels: 126 us -> 125 us  [body(): pl.pallas_call(kernel, out_shape=jax.ShapeDtypeStruct((512, 512), BF), in...]
where the time goes in v6:
time: 129 us; the launch traced here: 127 us
  Pallas kernels  125 us (97%)
  local copies, waits for them, and re-layouts  1.87 us (1%)
    pallas_call x1, Pallas kernels, body(): pl.pallas_call(kernel, out_shape=jax.ShapeDtypeStruct((512, 512), BF), in...  125 us

profile of v6, /device:TPU:1, one launch (start us, length us, event | category | flops | bytes accessed | tf_op | source)
XLA Modules:
  0.0 126.6 jit_solution(4014399172311946149)
XLA Ops:
  0.0 124.7 %shard_map.109 = bf16[512,512]{1,0:T(8,128)(2,1)} custom-call(bf16[512,512]{1,0:T(8,128)(2,1)} %hidden.1, bf16[4096]{0:T(1024)(128)(2,1)} %gain_in.1, bf16[8,64,128]{2,1,0:T(8,128)(2,1)} %bitcast.2, s32[8]{0:T(128)} %counts.1, s32[4,8]{1,0:T(4,128)} %bitcast.3, bf16[4096,256]{1,0:T(8,128)(2,1)} %w_skv.1, bf16[64,1024]{1,0:T(8,128)(2,1)} %w_eq.1, ...), custom_call_target="tpu_custom_call" | custom-call | flops 11000000512 | bytes 14000000 | tf_op jit(solution)/shard_map/pallas_call | solution.py:703
  124.7 1.9 %copy.13 = bf16[512,512]{1,0:T(8,128)(2,1)} copy(bf16[512,512]{1,0:T(8,128)(2,1)} %shard_map.109) | data formatting | bytes 1048576
